TPU v7x, 32 devices: a whole 2x2x4 slice. The times are simulated.
32 devices in a mesh: section: 16 (over z, y, x), tp: 2 (over core).
Axes of the slice: x: 2, y: 2, z: 4, core: 2. Of those that a mesh axis runs over, the one named last changes fastest.
Arguments:
- hidden_t: bfloat16 [8192, 384], P('tp'), may hold values from -40 to 40
- norm_gain: bfloat16 [4, 8192], replicated, may hold values from 0.099609375 to 1.8984375
- q_weight: bfloat16 [16, 8192, 512], P('section', None, 'tp'), may hold values from -0.0625 to 0.0625
- k_weight: bfloat16 [16, 2048, 256], P('section', None, 'tp'), may hold values from -0.0625 to 0.0625
- v_weight: bfloat16 [16, 2048, 256], P('section', None, 'tp'), may hold values from -0.0625 to 0.0625
- o_weight: bfloat16 [16, 512, 8192], P('section', 'tp'), may hold values from -0.125 to 0.125
- lengths: int32 [16], replicated, may hold values from 1 to 48, 384 in all
- prior_offsets: int32 [16], replicated, may hold values from 0 to 4095
- owners: int32 [16], replicated, may hold values from 0 to 15, each once
Outputs:
- final_hidden: bfloat16 [8192, 384], P('tp', 'section')
- kv_cache: bfloat16 [16, 4, 48, 512], P('section', None, None, 'tp')
Inputs may be any that keep to these rules, and one draw needn't show every extreme that they name: `lengths`: the 16 requests fill all 384 tokens; some request has exactly 48 tokens. `owners`: each owner serves exactly one request.
All inputs are finite; a program needn't handle non-finite values.
Results may differ from a plain program's by a relative error of at most 0.023.
Values may be sent and summed in bfloat16 or wider, within the bound.
A program may use at most 128 MiB of HBM per device.

v0:
```python
import math

import jax
import jax.numpy as jnp
from jax import lax
from jax.sharding import PartitionSpec as P

HEAD_DIM = 128
SUBS = 4


NORM_EPS = 1e-05
ROPE_BASE = 500000.0


def partner_2(shard, axis, distance):
    return lax.ppermute(shard, axis, [(i, i ^ 1 << distance) for i in range(lax.axis_size(axis))])


def from_behind(shard, axis, by):
    devices = lax.axis_size(axis)
    pairs = [(i, i + by) for i in range(devices) if 0 <= i + by < devices]
    return lax.ppermute(shard, axis, pairs)


def rope_tables(positions):
    half_dim = HEAD_DIM // 2
    steps_i = jnp.arange(half_dim, dtype=jnp.float32)
    inv_freq = jnp.power(jnp.float32(ROPE_BASE), -(2.0 * steps_i) / HEAD_DIM)
    angle = positions.astype(jnp.float32)[:, None] * inv_freq[None, :]
    return (jnp.cos(angle)[:, None, :], jnp.sin(angle)[:, None, :])


def rotate_pairs(values, cos_table, sin_table):
    half_dim = values.shape[-1] // 2
    first_half = values[..., :half_dim]
    second_half = values[..., half_dim:]
    return jnp.concatenate(
        [
            first_half * cos_table - second_half * sin_table,
            second_half * cos_table + first_half * sin_table,
        ],
        axis=-1,
    )


def group_total(values):
    for bit_num in range(SUBS.bit_length() - 1):
        partner = partner_2(values.astype(jnp.bfloat16), "section", bit_num).astype(values.dtype)
        values = values + partner
    return values


def shards(
    hidden_t, norm_gain, q_weight, k_weight, v_weight, o_weight, lengths, prior_offsets, owners
):
    section_count = lax.axis_size("section")
    section_idx = lax.axis_index("section")
    layer_count = section_count // SUBS
    layer_idx = section_idx // SUBS
    sub_idx = section_idx % SUBS
    rows_dev, tokens = hidden_t.shape
    num_reqs = lengths.shape[0]
    capacity = 2 * tokens // num_reqs
    quarter = capacity // SUBS
    pieces = 1
    span_cols = tokens // pieces
    gain_vec = lax.dynamic_index_in_dim(norm_gain, layer_idx, 0, keepdims=False).astype(jnp.float32)
    w_query = q_weight[0]
    w_key = k_weight[0]
    w_value = v_weight[0]
    w_out = o_weight[0]
    rows_sub = w_key.shape[0]
    groups = w_query.shape[1] // HEAD_DIM
    contract_first = (((0,), (0,)), ((), ()))
    req_ends = jnp.cumsum(lengths)
    req_starts = req_ends - lengths
    tok_ids = jnp.arange(tokens, dtype=jnp.int32)
    req_ids = jnp.arange(num_reqs, dtype=jnp.int32)
    req_of_tok = jnp.sum((tok_ids[:, None] >= req_ends[None, :]).astype(jnp.int32), axis=1)
    req_onehot = req_of_tok[:, None] == req_ids[None, :]
    positions = (
        jnp.sum(jnp.where(req_onehot, (prior_offsets - req_starts)[None, :], 0), axis=1) + tok_ids
    )
    key_mask = (req_of_tok[:, None] == req_of_tok[None, :]) & (tok_ids[None, :] <= tok_ids[:, None])
    cos_table, sin_table = rope_tables(positions)

    def project(whole):
        h_float = whole.astype(jnp.float32)
        mean_square = jnp.mean(h_float * h_float, axis=0)
        normed = (h_float * lax.rsqrt(mean_square + NORM_EPS)[None, :] * gain_vec[:, None]).astype(
            jnp.bfloat16
        )
        query_rows = lax.dot_general(
            normed, w_query, contract_first, preferred_element_type=jnp.float32
        )
        normed_sub = lax.dynamic_slice_in_dim(normed, sub_idx * rows_sub, rows_sub, 0)
        key_part = lax.dot_general(
            normed_sub, w_key, contract_first, preferred_element_type=jnp.float32
        )
        value_part = lax.dot_general(
            normed_sub, w_value, contract_first, preferred_element_type=jnp.float32
        )
        return (query_rows, jnp.concatenate([key_part, value_part], axis=1))

    def spare_project(whole):
        return (
            jnp.zeros((span_cols, groups * HEAD_DIM), jnp.float32),
            jnp.zeros((span_cols, 2 * HEAD_DIM), jnp.float32),
        )

    def attend(operands):
        query_rows, kv_total, kv_buf, col_start = operands
        key_rows = kv_total[:, :HEAD_DIM]
        value_rows = kv_total[:, HEAD_DIM:]
        query_rot = rotate_pairs(
            query_rows.reshape(span_cols, groups, HEAD_DIM), cos_table, sin_table
        ).astype(jnp.bfloat16)
        key_new = (
            rotate_pairs(key_rows.reshape(span_cols, 1, HEAD_DIM), cos_table, sin_table)
            .reshape(span_cols, HEAD_DIM)
            .astype(jnp.bfloat16)
        )
        value_new = value_rows.astype(jnp.bfloat16)
        kv_buf = jnp.concatenate([key_new, value_new], axis=1)
        scores = jnp.einsum(
            "wgh,th->gwt", query_rot, kv_buf[:, :HEAD_DIM], preferred_element_type=jnp.float32
        ) / math.sqrt(HEAD_DIM)
        exp_scores = jnp.where(key_mask[None], jnp.exp(scores), 0.0)
        probs = (exp_scores / jnp.sum(exp_scores, axis=-1, keepdims=True)).astype(jnp.bfloat16)
        attended = jnp.einsum(
            "gwt,th->wgh", probs, kv_buf[:, HEAD_DIM:], preferred_element_type=jnp.float32
        )
        attended = attended.astype(jnp.bfloat16).reshape(span_cols, groups * HEAD_DIM)
        return (attended, kv_buf)

    def spare_attend(operands):
        query_rows, kv_total, kv_buf, col_start = operands
        return (jnp.zeros((span_cols, groups * HEAD_DIM), jnp.bfloat16), kv_buf)

    def run_layer(piece_in, micro_idx, kv_buf, active):
        col_start = micro_idx * span_cols
        whole = lax.all_gather(piece_in, "tp", axis=0, tiled=True)
        query_rows, kv_part = lax.cond(active, project, spare_project, whole)
        kv_total = group_total(kv_part)
        attended, kv_buf = lax.cond(
            active, attend, spare_attend, (query_rows, kv_total, kv_buf, col_start)
        )
        row_count = rows_dev * lax.axis_size("tp")

        def full_term(cols_now):
            return lax.dot_general(
                cols_now, attended, (((0,), (1,)), ((), ())), preferred_element_type=jnp.float32
            )

        def empty_term(cols_now):
            return jnp.zeros((row_count, span_cols), jnp.float32)

        summed = lax.psum_scatter(
            lax.cond(active, full_term, empty_term, w_out).astype(jnp.bfloat16),
            "tp",
            scatter_dimension=0,
            tiled=True,
        ).astype(jnp.float32)
        summed = group_total(summed)
        updated = jnp.where(
            active,
            (piece_in.astype(jnp.float32) + summed).astype(jnp.bfloat16),
            jnp.zeros((), jnp.bfloat16),
        )
        return (updated, kv_buf)

    def step_fn(step_num, state_now):
        received, kv_buf, final_buf = state_now
        micro_raw = step_num - layer_idx
        active = (micro_raw >= 0) & (micro_raw < pieces)
        micro_idx = jnp.clip(micro_raw, 0, pieces - 1)
        piece_in = jnp.where(layer_idx == 0, hidden_t, received)
        updated, kv_buf = run_layer(piece_in, micro_idx, kv_buf, active)
        final_buf = jnp.where(active & (layer_idx == layer_count - 1), updated, final_buf)
        received = from_behind(updated, "section", SUBS)
        return (received, kv_buf, final_buf)

    start_state = (
        jnp.zeros((rows_dev, span_cols), jnp.bfloat16),
        jnp.zeros((tokens, 2 * HEAD_DIM), jnp.bfloat16),
        jnp.zeros((rows_dev, tokens), jnp.bfloat16),
    )
    received, kv_buf, final_buf = lax.fori_loop(0, layer_count + pieces - 1, step_fn, start_state)
    last_terms = jnp.where(
        (layer_idx == layer_count - 1) & (sub_idx == 0), final_buf.astype(jnp.float32), 0.0
    )
    final_hidden = lax.psum_scatter(
        last_terms.astype(jnp.bfloat16), "section", scatter_dimension=1, tiled=True
    )
    owner_onehot = owners[None, :] == req_ids[:, None]
    owner_starts = jnp.sum(jnp.where(owner_onehot, req_starts[None, :], 0), axis=1)
    owner_lens = jnp.sum(jnp.where(owner_onehot, lengths[None, :], 0), axis=1)
    slot_ids = jnp.arange(capacity, dtype=jnp.int32)
    row_index = jnp.minimum(owner_starts[:, None] + slot_ids[None, :], tokens - 1)
    row_valid = slot_ids[None, :] < owner_lens[:, None]
    own_select = req_ids == section_idx
    mine_index = jnp.sum(jnp.where(own_select[:, None], row_index, 0), axis=0)
    mine_valid = jnp.any(own_select[:, None] & row_valid, axis=0)
    slot_quarter = slot_ids // quarter
    piece_rows = lax.all_gather(kv_buf[None], "section", axis=0, tiled=True)
    count_now = piece_rows.shape[0]
    sources = jnp.arange(count_now, dtype=jnp.int32)
    keep_slot = (slot_quarter[None, :] == (sources % SUBS)[:, None]) & mine_valid[None, :]
    picked = jnp.where(
        keep_slot[:, :, None], piece_rows[:, mine_index], jnp.zeros((), jnp.bfloat16)
    )
    combined = jnp.sum(
        picked.reshape(layer_count, SUBS, capacity, 2 * HEAD_DIM).astype(jnp.float32), axis=1
    )
    kv_cache = combined.astype(jnp.bfloat16)[None]
    return (final_hidden, kv_cache)


def solution(mesh):
    return jax.shard_map(
        shards,
        mesh=mesh,
        in_specs=(
            P("tp", None),
            P(),
            P("section", None, "tp"),
            P("section", None, "tp"),
            P("section", None, "tp"),
            P("section", "tp", None),
            P(),
            P(),
            P(),
        ),
        out_specs=(P("tp", "section"), P("section", None, None, "tp")),
        check_vma=False,
    )
```

profile of v0, /device:TPU:28, one launch (start us, length us, event | category | flops | bytes accessed | tf_op | source)
XLA Modules:
  0.0 1432.7 jit_solution(15768822478687085732)
XLA Ops:
  12.3 1207.0 %while.24 = (s32[]{:T(128)}, bf16[4096,384]{1,0:T(8,128)(2,1)S(1)}, bf16[384,256]{1,0:T(8,128)(2,1)}, bf16[4096,384]{1,0:T(8,128)(2,1)}, s32[]{:T(128)}, /*index...) while((s32[]{:T(128)}, bf16[4096,384]{1,0:T(8,128)(2,1)S(1)}, ...), condition=%wide.region_13.14_spmd.clone.clone.clone, body=%wide.region_3.13_spmd.clone.clone.clone.sunk | while | flops 3826263552 | bytes 283782944 | solution.py:189
  14.4 18.2 %all-gather.6.cloned.1.call-done = bf16[8192,384]{1,0:T(8,128)(2,1)} async-done(((bf16[4096,384]{1,0:T(8,128)(2,1)}), bf16[8192,384]{1,0:T(8,128)(2,1)}) %all-gather.6.cloned.1.call-update) | async-done | bytes 6291472 | tf_op jit(solution)/shard_map/while/body/eval_jaxpr/all_gather | solution.py:143
  50.4 38.3 %reduce-scatter.5.cloned.1.call-done = bf16[4096,384]{1,0:T(8,128)(2,1)} async-done(((bf16[8192,384]{1,0:T(8,128)(2,1)}), bf16[4096,384]{1,0:T(8,128)(2,1)}) %reduce-scatter.5.cloned.1.call-update) | async-done | bytes 3145744 | tf_op jit(solution)/shard_map/while/body/eval_jaxpr/reduce_scatter | solution.py:159
  90.2 69.1 %collective-permute-done.2 = bf16[4096,384]{1,0:T(8,128)(2,1)S(1)} collective-permute-done((bf16[4096,384]{1,0:T(8,128)(2,1)}, bf16[4096,384]{1,0:T(8,128)(2,1)S(1)}, u32[]{:S(2)}, u32[]{:S(2)}) %collective-permute-start.2) | collective-permute-done | bytes 3145760 | tf_op jit(solution)/shard_map/while/body/eval_jaxpr/ppermute | solution.py:17
  165.4 69.3 %collective-permute-done.3 = bf16[4096,384]{1,0:T(8,128)(2,1)} collective-permute-done((bf16[4096,384]{1,0:T(8,128)(2,1)}, bf16[4096,384]{1,0:T(8,128)(2,1)}, u32[]{:S(2)}, u32[]{:S(2)}) %collective-permute-start.3) | collective-permute-done | bytes 3145760 | tf_op jit(solution)/shard_map/while/body/eval_jaxpr/ppermute | solution.py:17
  242.6 69.4 %collective-permute-done.4 = bf16[4096,384]{1,0:T(8,128)(2,1)S(1)} collective-permute-done((bf16[4096,384]{1,0:T(8,128)(2,1)}, bf16[4096,384]{1,0:T(8,128)(2,1)S(1)}, u32[]{:S(2)}, u32[]{:S(2)}) %collective-permute-start.4) | collective-permute-done | bytes 3145760 | tf_op jit(solution)/shard_map/while/body/eval_jaxpr/ppermute | solution.py:23
  314.1 18.2 %all-gather.6.cloned.1.call-done = bf16[8192,384]{1,0:T(8,128)(2,1)} async-done(((bf16[4096,384]{1,0:T(8,128)(2,1)}), bf16[8192,384]{1,0:T(8,128)(2,1)}) %all-gather.6.cloned.1.call-update) | async-done | bytes 6291472 | tf_op jit(solution)/shard_map/while/body/eval_jaxpr/all_gather | solution.py:143
  350.1 39.2 %reduce-scatter.5.cloned.1.call-done = bf16[4096,384]{1,0:T(8,128)(2,1)} async-done(((bf16[8192,384]{1,0:T(8,128)(2,1)}), bf16[4096,384]{1,0:T(8,128)(2,1)}) %reduce-scatter.5.cloned.1.call-update) | async-done | bytes 3145744 | tf_op jit(solution)/shard_map/while/body/eval_jaxpr/reduce_scatter | solution.py:159
  390.8 69.1 %collective-permute-done.2 = bf16[4096,384]{1,0:T(8,128)(2,1)S(1)} collective-permute-done((bf16[4096,384]{1,0:T(8,128)(2,1)}, bf16[4096,384]{1,0:T(8,128)(2,1)S(1)}, u32[]{:S(2)}, u32[]{:S(2)}) %collective-permute-start.2) | collective-permute-done | bytes 3145760 | tf_op jit(solution)/shard_map/while/body/eval_jaxpr/ppermute | solution.py:17
  466.0 69.3 %collective-permute-done.3 = bf16[4096,384]{1,0:T(8,128)(2,1)} collective-permute-done((bf16[4096,384]{1,0:T(8,128)(2,1)}, bf16[4096,384]{1,0:T(8,128)(2,1)}, u32[]{:S(2)}, u32[]{:S(2)}) %collective-permute-start.3) | collective-permute-done | bytes 3145760 | tf_op jit(solution)/shard_map/while/body/eval_jaxpr/ppermute | solution.py:17
  544.1 69.4 %collective-permute-done.4 = bf16[4096,384]{1,0:T(8,128)(2,1)S(1)} collective-permute-done((bf16[4096,384]{1,0:T(8,128)(2,1)}, bf16[4096,384]{1,0:T(8,128)(2,1)S(1)}, u32[]{:S(2)}, u32[]{:S(2)}) %collective-permute-start.4) | collective-permute-done | bytes 3145760 | tf_op jit(solution)/shard_map/while/body/eval_jaxpr/ppermute | solution.py:23
  615.7 18.0 %all-gather.6.cloned.1.call-done = bf16[8192,384]{1,0:T(8,128)(2,1)} async-done(((bf16[4096,384]{1,0:T(8,128)(2,1)}), bf16[8192,384]{1,0:T(8,128)(2,1)}) %all-gather.6.cloned.1.call-update) | async-done | bytes 6291472 | tf_op jit(solution)/shard_map/while/body/eval_jaxpr/all_gather | solution.py:143
  651.5 40.2 %reduce-scatter.5.cloned.1.call-done = bf16[4096,384]{1,0:T(8,128)(2,1)} async-done(((bf16[8192,384]{1,0:T(8,128)(2,1)}), bf16[4096,384]{1,0:T(8,128)(2,1)}) %reduce-scatter.5.cloned.1.call-update) | async-done | bytes 3145744 | tf_op jit(solution)/shard_map/while/body/eval_jaxpr/reduce_scatter | solution.py:159
  693.1 69.1 %collective-permute-done.2 = bf16[4096,384]{1,0:T(8,128)(2,1)S(1)} collective-permute-done((bf16[4096,384]{1,0:T(8,128)(2,1)}, bf16[4096,384]{1,0:T(8,128)(2,1)S(1)}, u32[]{:S(2)}, u32[]{:S(2)}) %collective-permute-start.2) | collective-permute-done | bytes 3145760 | tf_op jit(solution)/shard_map/while/body/eval_jaxpr/ppermute | solution.py:17
  768.3 69.3 %collective-permute-done.3 = bf16[4096,384]{1,0:T(8,128)(2,1)} collective-permute-done((bf16[4096,384]{1,0:T(8,128)(2,1)}, bf16[4096,384]{1,0:T(8,128)(2,1)}, u32[]{:S(2)}, u32[]{:S(2)}) %collective-permute-start.3) | collective-permute-done | bytes 3145760 | tf_op jit(solution)/shard_map/while/body/eval_jaxpr/ppermute | solution.py:17
  846.4 69.4 %collective-permute-done.4 = bf16[4096,384]{1,0:T(8,128)(2,1)S(1)} collective-permute-done((bf16[4096,384]{1,0:T(8,128)(2,1)}, bf16[4096,384]{1,0:T(8,128)(2,1)S(1)}, u32[]{:S(2)}, u32[]{:S(2)}) %collective-permute-start.4) | collective-permute-done | bytes 3145760 | tf_op jit(solution)/shard_map/while/body/eval_jaxpr/ppermute | solution.py:23
  918.0 18.2 %all-gather.6.cloned.1.call-done = bf16[8192,384]{1,0:T(8,128)(2,1)} async-done(((bf16[4096,384]{1,0:T(8,128)(2,1)}), bf16[8192,384]{1,0:T(8,128)(2,1)}) %all-gather.6.cloned.1.call-update) | async-done | bytes 6291472 | tf_op jit(solution)/shard_map/while/body/eval_jaxpr/all_gather | solution.py:143
  936.2 17.2 %conditional.15 = (f32[384,256]{1,0:T(8,128)S(1)}, f32[384,256]{1,0:T(8,128)S(1)}) conditional(s32[]{:T(128)} %convert_element_type.250, () %tuple.123, (bf16[8192,384]{1,0:T(8,128)(2,1)}, f32[8192]{0:T(1024)S(1)}, bf16[8192,256]{1,0:T(8,128)(2,1)}, s32[]{:T(128)}, bf16[2048,128]{1,0:T(8,128)(2,1)S(1)}, ...), branch_computations={%region_4.4_spmd, %region_5.6_spmd} | conditional | flops 2035384704 | bytes 86284400 | solution.py:144
  979.3 15.8 %reduce-scatter.5.cloned.1.call-done = bf16[4096,384]{1,0:T(8,128)(2,1)} async-done(((bf16[8192,384]{1,0:T(8,128)(2,1)}), bf16[4096,384]{1,0:T(8,128)(2,1)}) %reduce-scatter.5.cloned.1.call-update) | async-done | bytes 3145744 | tf_op jit(solution)/shard_map/while/body/eval_jaxpr/reduce_scatter | solution.py:159
  996.6 69.1 %collective-permute-done.2 = bf16[4096,384]{1,0:T(8,128)(2,1)S(1)} collective-permute-done((bf16[4096,384]{1,0:T(8,128)(2,1)}, bf16[4096,384]{1,0:T(8,128)(2,1)S(1)}, u32[]{:S(2)}, u32[]{:S(2)}) %collective-permute-start.2) | collective-permute-done | bytes 3145760 | tf_op jit(solution)/shard_map/while/body/eval_jaxpr/ppermute | solution.py:17
  1071.7 69.3 %collective-permute-done.3 = bf16[4096,384]{1,0:T(8,128)(2,1)} collective-permute-done((bf16[4096,384]{1,0:T(8,128)(2,1)}, bf16[4096,384]{1,0:T(8,128)(2,1)}, u32[]{:S(2)}, u32[]{:S(2)}) %collective-permute-start.3) | collective-permute-done | bytes 3145760 | tf_op jit(solution)/shard_map/while/body/eval_jaxpr/ppermute | solution.py:17
  1149.9 69.4 %collective-permute-done.4 = bf16[4096,384]{1,0:T(8,128)(2,1)S(1)} collective-permute-done((bf16[4096,384]{1,0:T(8,128)(2,1)}, bf16[4096,384]{1,0:T(8,128)(2,1)S(1)}, u32[]{:S(2)}, u32[]{:S(2)}) %collective-permute-start.4) | collective-permute-done | bytes 3145760 | tf_op jit(solution)/shard_map/while/body/eval_jaxpr/ppermute | solution.py:23
  1227.3 62.6 %all-gather.4.cloned.1.call-done = bf16[6144,256]{1,0:T(8,128)(2,1)} async-done(((bf16[384,256]{1,0:T(8,128)(2,1)}), bf16[6144,256]{1,0:T(8,128)(2,1)}) %all-gather.4.cloned.1.call-update) | async-done | bytes 3145744 | tf_op jit(solution)/shard_map/all_gather | solution.py:206
  1296.2 129.1 %reduce-scatter.3.cloned.1.call-done = bf16[4096,24]{0,1:T(8,128)(2,1)} async-done(((bf16[4096,384]{0,1:T(8,128)(2,1)}), bf16[4096,24]{0,1:T(8,128)(2,1)}) %reduce-scatter.3.cloned.1.call-update) | async-done | bytes 196624 | tf_op jit(solution)/shard_map/reduce_scatter | solution.py:193
  (238 shorter events, 208.6 us)
Async XLA Ops:
  12.3 20.4 %all-gather.6.cloned.1.call-start = ((), (), s32[]{:S(2)}) async-start(), calls=%async_computation.4 | async-start | bytes 9437184 | tf_op jit(solution)/shard_map/while/body/eval_jaxpr/all_gather | solution.py:143
  14.3 74.5 %reduce-scatter.5.cloned.1.call-start = ((), (), s32[]{:S(2)}) async-start(), calls=%async_computation.5 | async-start | bytes 9437184 | tf_op jit(solution)/shard_map/while/body/eval_jaxpr/reduce_scatter | solution.py:159
  32.7 7.2 collective-permute-start
  88.8 70.5 %collective-permute-start.2 = (bf16[4096,384]{1,0:T(8,128)(2,1)}, bf16[4096,384]{1,0:T(8,128)(2,1)S(1)}, u32[]{:S(2)}, u32[]{:S(2)}) collective-permute-start(bf16[4096,384]{1,0:T(8,128)(2,1)} %reduce-scatter.5.cloned.1.call-done), channel_id=1, source_target_pairs={{0,2},{2,0},{4,6},{6,4},{8,10},{10,8},{12,14},{14,12},{16,18},{18,... | collective-permute-start | bytes 9437192 | tf_op jit(solution)/shard_map/while/body/eval_jaxpr/ppermute | solution.py:17
  164.8 69.8 %collective-permute-start.3 = (bf16[4096,384]{1,0:T(8,128)(2,1)}, bf16[4096,384]{1,0:T(8,128)(2,1)}, u32[]{:S(2)}, u32[]{:S(2)}) collective-permute-start(bf16[4096,384]{1,0:T(8,128)(2,1)} %fusion.52), channel_id=1, source_target_pairs={{0,4},{2,6},{4,0},{6,2},{8,12},{10,14},{12,8},{14,10},{16,20},{18,... | collective-permute-start | bytes 9437192 | tf_op jit(solution)/shard_map/while/body/eval_jaxpr/ppermute | solution.py:17
  241.3 70.7 %collective-permute-start.4 = (bf16[4096,384]{1,0:T(8,128)(2,1)}, bf16[4096,384]{1,0:T(8,128)(2,1)S(1)}, u32[]{:S(2)}, u32[]{:S(2)}) collective-permute-start(bf16[4096,384]{1,0:T(8,128)(2,1)} %get-tuple-element.765), channel_id=1, source_target_pairs={{0,8},{2,10},{4,12},{6,14},{8,16},{10,18},{12,20},{14,22},{16,24},... | collective-permute-start | bytes 9437192 | tf_op jit(solution)/shard_map/while/body/eval_jaxpr/ppermute | solution.py:23
  312.0 20.3 %all-gather.6.cloned.1.call-start = ((), (), s32[]{:S(2)}) async-start(), calls=%async_computation.4 | async-start | bytes 9437184 | tf_op jit(solution)/shard_map/while/body/eval_jaxpr/all_gather | solution.py:143
  314.0 75.3 %reduce-scatter.5.cloned.1.call-start = ((), (), s32[]{:S(2)}) async-start(), calls=%async_computation.5 | async-start | bytes 9437184 | tf_op jit(solution)/shard_map/while/body/eval_jaxpr/reduce_scatter | solution.py:159
  389.4 70.5 %collective-permute-start.2 = (bf16[4096,384]{1,0:T(8,128)(2,1)}, bf16[4096,384]{1,0:T(8,128)(2,1)S(1)}, u32[]{:S(2)}, u32[]{:S(2)}) collective-permute-start(bf16[4096,384]{1,0:T(8,128)(2,1)} %reduce-scatter.5.cloned.1.call-done), channel_id=1, source_target_pairs={{0,2},{2,0},{4,6},{6,4},{8,10},{10,8},{12,14},{14,12},{16,18},{18,... | collective-permute-start | bytes 9437192 | tf_op jit(solution)/shard_map/while/body/eval_jaxpr/ppermute | solution.py:17
  465.4 69.8 %collective-permute-start.3 = (bf16[4096,384]{1,0:T(8,128)(2,1)}, bf16[4096,384]{1,0:T(8,128)(2,1)}, u32[]{:S(2)}, u32[]{:S(2)}) collective-permute-start(bf16[4096,384]{1,0:T(8,128)(2,1)} %fusion.52), channel_id=1, source_target_pairs={{0,4},{2,6},{4,0},{6,2},{8,12},{10,14},{12,8},{14,10},{16,20},{18,... | collective-permute-start | bytes 9437192 | tf_op jit(solution)/shard_map/while/body/eval_jaxpr/ppermute | solution.py:17
  542.8 70.7 %collective-permute-start.4 = (bf16[4096,384]{1,0:T(8,128)(2,1)}, bf16[4096,384]{1,0:T(8,128)(2,1)S(1)}, u32[]{:S(2)}, u32[]{:S(2)}) collective-permute-start(bf16[4096,384]{1,0:T(8,128)(2,1)} %get-tuple-element.765), channel_id=1, source_target_pairs={{0,8},{2,10},{4,12},{6,14},{8,16},{10,18},{12,20},{14,22},{16,24},... | collective-permute-start | bytes 9437192 | tf_op jit(solution)/shard_map/while/body/eval_jaxpr/ppermute | solution.py:23
  613.6 20.1 %all-gather.6.cloned.1.call-start = ((), (), s32[]{:S(2)}) async-start(), calls=%async_computation.4 | async-start | bytes 9437184 | tf_op jit(solution)/shard_map/while/body/eval_jaxpr/all_gather | solution.py:143
  615.6 76.1 %reduce-scatter.5.cloned.1.call-start = ((), (), s32[]{:S(2)}) async-start(), calls=%async_computation.5 | async-start | bytes 9437184 | tf_op jit(solution)/shard_map/while/body/eval_jaxpr/reduce_scatter | solution.py:159
  633.8 7.2 collective-permute-start
  691.7 70.5 %collective-permute-start.2 = (bf16[4096,384]{1,0:T(8,128)(2,1)}, bf16[4096,384]{1,0:T(8,128)(2,1)S(1)}, u32[]{:S(2)}, u32[]{:S(2)}) collective-permute-start(bf16[4096,384]{1,0:T(8,128)(2,1)} %reduce-scatter.5.cloned.1.call-done), channel_id=1, source_target_pairs={{0,2},{2,0},{4,6},{6,4},{8,10},{10,8},{12,14},{14,12},{16,18},{18,... | collective-permute-start | bytes 9437192 | tf_op jit(solution)/shard_map/while/body/eval_jaxpr/ppermute | solution.py:17
  767.7 69.8 %collective-permute-start.3 = (bf16[4096,384]{1,0:T(8,128)(2,1)}, bf16[4096,384]{1,0:T(8,128)(2,1)}, u32[]{:S(2)}, u32[]{:S(2)}) collective-permute-start(bf16[4096,384]{1,0:T(8,128)(2,1)} %fusion.52), channel_id=1, source_target_pairs={{0,4},{2,6},{4,0},{6,2},{8,12},{10,14},{12,8},{14,10},{16,20},{18,... | collective-permute-start | bytes 9437192 | tf_op jit(solution)/shard_map/while/body/eval_jaxpr/ppermute | solution.py:17
  845.2 70.7 %collective-permute-start.4 = (bf16[4096,384]{1,0:T(8,128)(2,1)}, bf16[4096,384]{1,0:T(8,128)(2,1)S(1)}, u32[]{:S(2)}, u32[]{:S(2)}) collective-permute-start(bf16[4096,384]{1,0:T(8,128)(2,1)} %get-tuple-element.765), channel_id=1, source_target_pairs={{0,8},{2,10},{4,12},{6,14},{8,16},{10,18},{12,20},{14,22},{16,24},... | collective-permute-start | bytes 9437192 | tf_op jit(solution)/shard_map/while/body/eval_jaxpr/ppermute | solution.py:23
  915.9 20.3 %all-gather.6.cloned.1.call-start = ((), (), s32[]{:S(2)}) async-start(), calls=%async_computation.4 | async-start | bytes 9437184 | tf_op jit(solution)/shard_map/while/body/eval_jaxpr/all_gather | solution.py:143
  917.9 77.2 %reduce-scatter.5.cloned.1.call-start = ((), (), s32[]{:S(2)}) async-start(), calls=%async_computation.5 | async-start | bytes 9437184 | tf_op jit(solution)/shard_map/while/body/eval_jaxpr/reduce_scatter | solution.py:159
  995.1 70.5 %collective-permute-start.2 = (bf16[4096,384]{1,0:T(8,128)(2,1)}, bf16[4096,384]{1,0:T(8,128)(2,1)S(1)}, u32[]{:S(2)}, u32[]{:S(2)}) collective-permute-start(bf16[4096,384]{1,0:T(8,128)(2,1)} %reduce-scatter.5.cloned.1.call-done), channel_id=1, source_target_pairs={{0,2},{2,0},{4,6},{6,4},{8,10},{10,8},{12,14},{14,12},{16,18},{18,... | collective-permute-start | bytes 9437192 | tf_op jit(solution)/shard_map/while/body/eval_jaxpr/ppermute | solution.py:17
  1071.2 69.8 %collective-permute-start.3 = (bf16[4096,384]{1,0:T(8,128)(2,1)}, bf16[4096,384]{1,0:T(8,128)(2,1)}, u32[]{:S(2)}, u32[]{:S(2)}) collective-permute-start(bf16[4096,384]{1,0:T(8,128)(2,1)} %fusion.52), channel_id=1, source_target_pairs={{0,4},{2,6},{4,0},{6,2},{8,12},{10,14},{12,8},{14,10},{16,20},{18,... | collective-permute-start | bytes 9437192 | tf_op jit(solution)/shard_map/while/body/eval_jaxpr/ppermute | solution.py:17
  1148.6 70.7 %collective-permute-start.4 = (bf16[4096,384]{1,0:T(8,128)(2,1)}, bf16[4096,384]{1,0:T(8,128)(2,1)S(1)}, u32[]{:S(2)}, u32[]{:S(2)}) collective-permute-start(bf16[4096,384]{1,0:T(8,128)(2,1)} %get-tuple-element.765), channel_id=1, source_target_pairs={{0,8},{2,10},{4,12},{6,14},{8,16},{10,18},{12,20},{14,22},{16,24},... | collective-permute-start | bytes 9437192 | tf_op jit(solution)/shard_map/while/body/eval_jaxpr/ppermute | solution.py:23
  1219.3 70.6 %all-gather.4.cloned.1.call-start = ((), (), s32[]{:S(2)}) async-start(), calls=%async_computation.3 | async-start | bytes 3342336 | tf_op jit(solution)/shard_map/all_gather | solution.py:206
  1219.9 205.4 %reduce-scatter.3.cloned.1.call-start = ((), (), s32[]{:S(2)}) async-start(), calls=%async_computation.2 | async-start | bytes 3342336 | tf_op jit(solution)/shard_map/reduce_scatter | solution.py:193
  (45 other events, 1387.5 us)
Sparse Core Ops, SparseCore 0:
  14.6 17.9 all-gather.5
  50.5 38.1 reduce-scatter.4
  314.3 17.9 all-gather.5
  350.2 39.0 reduce-scatter.4
  615.7 17.9 all-gather.5
  651.6 40.0 reduce-scatter.4
  918.2 17.9 all-gather.5
  979.4 15.6 reduce-scatter.4
Sparse Core Ops, SparseCore 1:
  1222.5 67.3 all-gather.3
  1295.3 130.0 reduce-scatter.2
where the time goes:
time: 1440 us; the launch traced here: 1430 us
  waiting for transfers between devices  1270 us (88%)
  other arithmetic  76 us (5%)
  local copies, waits for them, and re-layouts  28.6 us (2%)
  starting transfers between devices  22 us (2%)
  between operations  15.6 us (1%)
  matrix products  14.9 us (1%)
    ppermute x16, waiting for transfers between devices, partner_2(): lax.ppermute(shard, axis, [(i, i ^ 1 << distance) for i in range(lax.axis...  598 us
    ppermute x4, waiting for transfers between devices, from_behind(): return lax.ppermute(shard, axis, pairs)  278 us
    reduce_scatter x4, waiting for transfers between devices, run_layer(): lax.psum_scatter(lax.cond(active, full_term, empty_term, w_out).astype(jn...  134 us
    reduce_scatter x1, waiting for transfers between devices, shards(): lax.psum_scatter(last_terms.astype(jnp.bfloat16), 'section', scatter_dime...  129 us
    all_gather x4, waiting for transfers between devices, run_layer(): whole = lax.all_gather(piece_in, 'tp', axis=0, tiled=True)  72.7 us
    all_gather x1, waiting for transfers between devices, shards(): piece_rows = lax.all_gather(kv_buf[None], 'section', axis=0, tiled=True)  62.6 us
    select_n x4, other arithmetic, step_fn(): jnp.where(active & (layer_idx == layer_count - 1), updated, final_buf)  29.4 us
  transfers between devices with their start and end apart: 30, of which 30 were waited for; matrix products, arithmetic and copies ran while one was open for 1% of the time, Pallas kernels for 0%

commit v1 on v0

v1 whole, which is shorter than its diff:
```python
import functools
import math

import jax
import jax.numpy as jnp
from jax import lax
from jax.experimental import pallas as pl
from jax.experimental.pallas import tpu as pltpu
from jax.sharding import PartitionSpec as P

HEAD_DIM = 128
SUBS = 4
BLOCK = 256
LAG = 2
NORM_EPS = 1e-05
ROPE_BASE = 500000.0
MESH = pl.DeviceIdType.MESH
F32 = jnp.float32
BF16 = jnp.bfloat16


def dot(a, b):
    return jnp.dot(a, b, preferred_element_type=F32)


def round_up(count, unit):
    return (count + unit - 1) // unit * unit


def relay_kernel(
    layers, tps, own_tokens,
    hin, gain, wq, wk, wv, wo, cosf, sinf, mask, pick,
    fin_out, kv_out,
    hbuf, qacc, kvacc, sumsq, kvst, kvrecv, kvb, att,
    s1out, s1in, s1own, s2in, upd, totf, fst, fin, pickst, kvbuf,
    hs, fwd_s, ag_s, kvp_s, kvp_r, s1_s, s1_r, s2_s, s2_r, z_s, pk_s, pk_r, fin_s, fin_r,
):
    section = lax.axis_index("section")
    t = lax.axis_index("tp")
    layer = section // SUBS
    u = section % SUBS
    chunks = hbuf.shape[1]
    tokens = hbuf.shape[2]
    depth = hbuf.shape[0] * chunks * BLOCK
    own = u * tps + t
    sections = layers * SUBS
    last = layers - 1
    out_tp = own // SUBS
    out_slot = own % SUBS
    base = layer * SUBS

    def copy(src, dst, send, recv, sec, core):
        return pltpu.make_async_remote_copy(
            src_ref=src, dst_ref=dst, send_sem=send, recv_sem=recv,
            device_id=(sec, core), device_id_type=MESH,
        )

    def sub_at(r):
        return (u + r) % SUBS

    def tp_at(e):
        return (t + e) % tps

    def first_copy(j, ci, e):
        p = t * SUBS + j
        return copy(hin.at[j, ci], hbuf.at[p, ci], fwd_s.at[j, ci, e - 1], hs.at[p, ci], section, tp_at(e))

    def fwd_copy(r, ci, e):
        p = sub_at(r) * tps + t
        return copy(hbuf.at[p, ci], hbuf.at[p, ci], fwd_s.at[r, ci, e - 1], hs.at[p, ci], section, tp_at(e))

    def ag_copy(r, ci):
        return copy(hbuf.at[own, ci], hbuf.at[own, ci], ag_s.at[r - 1, ci], hs.at[own, ci], base + sub_at(r), t)

    def wait_block(p, ci):
        copy(hbuf.at[p, ci], hbuf.at[p, ci], fwd_s.at[0, 0, 0], hs.at[p, ci], section, tp_at(1)).wait_recv()

    def kvp_copy(r):
        return copy(kvst, kvrecv.at[r - 1], kvp_s.at[r - 1], kvp_r.at[r - 1], base + sub_at(r), t)

    def s1_copy(r, ci, e):
        return copy(s1out.at[r, ci, e - 1], s1in.at[r, ci, e - 1], s1_s.at[r, ci, e - 1], s1_r.at[r, ci, e - 1],
                    section, tp_at(e))

    def s2_copy(r, ci):
        return copy(s1own.at[r, ci], s2in.at[r - 1, ci], s2_s.at[r - 1, ci], s2_r.at[r - 1, ci], base + sub_at(r), t)

    def z_copy(ci):
        return copy(upd.at[ci], hbuf.at[own, ci], z_s.at[ci], hs.at[own, ci], section + SUBS, t)

    def pick_copy(j):
        return copy(pickst.at[j], kvbuf.at[layer], pk_s.at[j], pk_r.at[layer], j * SUBS + u, t)

    def fin_copy(s):
        return copy(fst.at[s], fin.at[out_slot], fin_s.at[s], fin_r.at[out_slot], s, out_tp)

    def loop(count, body):
        def step(k, carry):
            body(k)
            return carry
        lax.fori_loop(0, count, step, jnp.int32(0))

    barrier = pltpu.get_barrier_semaphore()

    def greet(sec, core):
        pl.semaphore_signal(barrier, inc=1, device_id=(sec, core), device_id_type=MESH)

    for e in range(1, tps):
        greet(section, tp_at(e))
    for r in range(1, SUBS):
        greet(base + sub_at(r), t)
    for j in range(1, layers):
        greet((layer + j) % layers * SUBS + u, t)
    for j in range(SUBS):
        p = t * SUBS + j
        sec, core = last * SUBS + p // tps, p % tps

        @pl.when((sec != section) | (core != t))
        def _():
            greet(sec, core)

    spread_to = jnp.where(layer == last, sections - jnp.where(out_tp == t, 1, 0), 0)
    pl.semaphore_wait(barrier, (tps - 1) + (SUBS - 1) + (layers - 1) + spread_to)

    qacc[...] = jnp.zeros_like(qacc)
    kvacc[...] = jnp.zeros_like(kvacc)
    sumsq[...] = jnp.zeros_like(sumsq)
    totf[...] = jnp.zeros_like(totf)

    @pl.when(layer == 0)
    def _():
        def send(k):
            j, ci = k // chunks, k % chunks
            for e in range(1, tps):
                first_copy(j, ci, e).start()
            hbuf[t * SUBS + j, ci] = hin[j, ci]
        loop(SUBS * chunks, send)

        def arrive(k):
            j, ci = k // chunks, k % chunks
            for e in range(1, tps):
                wait_block(tp_at(e) * SUBS + j, ci)
        loop(SUBS * chunks, arrive)

    @pl.when(layer > 0)
    def _():
        def spread(ci):
            wait_block(own, ci)
            for r in range(1, SUBS):
                ag_copy(r, ci).start()
            for e in range(1, tps):
                fwd_copy(0, ci, e).start()
        loop(chunks, spread)

    def absorb(p, ci):
        x = hbuf[p, ci].astype(F32)
        sq = x * x
        part = sq[:, :HEAD_DIM]
        for i in range(1, BLOCK // HEAD_DIM):
            part = part + sq[:, i * HEAD_DIM:(i + 1) * HEAD_DIM]
        sumsq[...] += part
        scaled = (x * gain[p * chunks + ci]).astype(BF16)
        rows = pl.ds(pl.multiple_of((p * chunks + ci) * BLOCK, BLOCK), BLOCK)
        qacc[...] += dot(scaled, wq[rows, :])
        return scaled

    def near(k):
        ci, e = k // tps, k % tps
        d = tp_at(e)

        @pl.when((layer > 0) & (e > 0))
        def _():
            wait_block(u * tps + d, ci)
        scaled = absorb(u * tps + d, ci)
        rows = pl.ds(pl.multiple_of((d * chunks + ci) * BLOCK, BLOCK), BLOCK)
        kvacc[...] += dot(scaled, jnp.concatenate([wk[rows, :], wv[rows, :]], axis=1))
    loop(chunks * tps, near)

    kvst[...] = kvacc[...].astype(BF16)
    for r in range(1, SUBS):
        kvp_copy(r).start()

    def across(k):
        ci, r = k // (SUBS - 1), k % (SUBS - 1) + 1
        p = sub_at(r) * tps + t

        @pl.when(layer > 0)
        def _():
            wait_block(p, ci)
            for e in range(1, tps):
                fwd_copy(r, ci, e).start()
        absorb(p, ci)
    loop(chunks * (SUBS - 1), across)

    def far(k):
        ci, r = k // (SUBS - 1), k % (SUBS - 1) + 1
        for e in range(1, tps):
            p = sub_at(r) * tps + tp_at(e)

            @pl.when(layer > 0)
            def _():
                wait_block(p, ci)
            absorb(p, ci)
    loop(chunks * (SUBS - 1), far)

    scale = lax.rsqrt(jnp.sum(sumsq[...], axis=1, keepdims=True) / depth + NORM_EPS)
    kv = kvacc[...]
    for r in range(1, SUBS):
        kvp_copy(r).wait_recv()
        kv = kv + kvrecv[r - 1].astype(F32)
    kv = kv * scale

    def rotate(x):
        return x * cosf[...] + pltpu.roll(x, HEAD_DIM // 2, 1) * sinf[...]

    kvb[:, :HEAD_DIM] = rotate(kv[:, :HEAD_DIM]).astype(BF16)
    kvb[:, HEAD_DIM:] = kv[:, HEAD_DIM:].astype(BF16)
    for g in range(att.shape[1] // HEAD_DIM):
        cols = slice(g * HEAD_DIM, (g + 1) * HEAD_DIM)
        query = rotate(qacc[:, cols] * scale).astype(BF16)
        scores = lax.dot_general(
            query, kvb[:, :HEAD_DIM], (((1,), (1,)), ((), ())), preferred_element_type=F32
        ) * (1.0 / math.sqrt(HEAD_DIM))
        weights = jnp.where(mask[...] > 0.0, jnp.exp(scores), 0.0)
        probs = (weights / jnp.sum(weights, axis=1, keepdims=True)).astype(BF16)
        att[:, cols] = dot(probs, kvb[:, HEAD_DIM:]).astype(BF16)

    def term(p, ci):
        cols = pl.ds(pl.multiple_of((p * chunks + ci) * BLOCK, BLOCK), BLOCK)
        return dot(att[...], wo[:, cols]).astype(BF16)

    steps = chunks * SUBS

    def project(k):
        @pl.when(k < steps)
        def _():
            ci, r = k // SUBS, (k + 1) % SUBS
            v = sub_at(r)
            for e in range(1, tps):
                s1out[r, ci, e - 1] = term(v * tps + tp_at(e), ci)
                s1_copy(r, ci, e).start()
            s1own[r, ci] = term(v * tps + t, ci)

        @pl.when(k >= LAG)
        def _():
            ci, r = (k - LAG) // SUBS, (k - LAG + 1) % SUBS
            total = s1own[r, ci].astype(F32)
            for e in range(1, tps):
                s1_copy(r, ci, e).wait_recv()
                total = total + s1in[r, ci, e - 1].astype(F32)
            s1own[r, ci] = total.astype(BF16)

            @pl.when(r > 0)
            def _():
                s2_copy(r, ci).start()
    loop(steps + LAG, project)

    def deliver(j):
        pickst[j] = dot(pick[j], kvb[...]).astype(BF16)

        @pl.when(j == layer)
        def _():
            kvbuf[layer] = pickst[j]

        @pl.when(j != layer)
        def _():
            pick_copy(j).start()
    loop(layers, deliver)

    def finish(ci):
        total = hbuf[own, ci].astype(F32)
        terms = s1own[0, ci].astype(F32)
        for r in range(1, SUBS):
            s2_copy(r, ci).wait_recv()
            terms = terms + s2in[r - 1, ci].astype(F32)
        total = total + terms

        @pl.when(layer < last)
        def _():
            upd[ci] = total.astype(BF16)
            z_copy(ci).start()

        @pl.when(layer == last)
        def _():
            totf[:tokens] = total
            for s in range(sections):
                fst[s, ci] = totf[s * own_tokens:s * own_tokens + fst.shape[2]].astype(BF16)
    loop(chunks, finish)

    @pl.when(layer == last)
    def _():
        def out(s):
            mine = (s == section) & (out_tp == t)

            @pl.when(mine)
            def _():
                fin[out_slot] = fst[s]

            @pl.when(jnp.logical_not(mine))
            def _():
                fin_copy(s).start()
        loop(sections, out)

    def kv_in(j):
        @pl.when(j != layer)
        def _():
            copy(pickst.at[j], kvbuf.at[j], pk_s.at[j], pk_r.at[j], j * SUBS + u, t).wait_recv()
    loop(layers, kv_in)
    kv_out[...] = kvbuf[...]

    def fin_in(j):
        p = t * SUBS + j
        sec, core = last * SUBS + p // tps, p % tps

        @pl.when((sec != section) | (core != t))
        def _():
            copy(fst.at[0], fin.at[j], fin_s.at[0], fin_r.at[j], sec, core).wait_recv()
    loop(SUBS, fin_in)
    fin_out[...] = fin[...]

    @pl.when(layer == 0)
    def _():
        def sent(k):
            for e in range(1, tps):
                first_copy(k // chunks, k % chunks, e).wait_send()
        loop(SUBS * chunks, sent)

    @pl.when(layer > 0)
    def _():
        def sent(ci):
            for r in range(SUBS):
                for e in range(1, tps):
                    fwd_copy(r, ci, e).wait_send()
            for r in range(1, SUBS):
                ag_copy(r, ci).wait_send()
        loop(chunks, sent)

    for r in range(1, SUBS):
        kvp_copy(r).wait_send()

    def sums_sent(ci):
        for r in range(SUBS):
            for e in range(1, tps):
                s1_copy(r, ci, e).wait_send()
        for r in range(1, SUBS):
            s2_copy(r, ci).wait_send()

        @pl.when(layer < last)
        def _():
            z_copy(ci).wait_send()
    loop(chunks, sums_sent)

    def kv_sent(j):
        @pl.when(j != layer)
        def _():
            pick_copy(j).wait_send()
    loop(layers, kv_sent)

    @pl.when(layer == last)
    def _():
        def sent(s):
            @pl.when(jnp.logical_not((s == section) & (out_tp == t)))
            def _():
                fin_copy(s).wait_send()
        loop(sections, sent)


def shards(
    hidden_t, norm_gain, q_weight, k_weight, v_weight, o_weight, lengths, prior_offsets, owners
):
    sections = lax.axis_size("section")
    tps = lax.axis_size("tp")
    section = lax.axis_index("section")
    layers = sections // SUBS
    layer = section // SUBS
    sub = section % SUBS
    rows_dev, tokens = hidden_t.shape
    num_reqs = lengths.shape[0]
    capacity = 2 * tokens // num_reqs
    cap_pad = round_up(capacity, 16)
    own_tokens = tokens // sections
    tok_pad = round_up(own_tokens, 16)
    pieces = SUBS * tps
    chunks = rows_dev // SUBS // BLOCK
    q_cols = q_weight.shape[2]

    req_ends = jnp.cumsum(lengths)
    req_starts = req_ends - lengths
    tok_ids = jnp.arange(tokens, dtype=jnp.int32)
    req_ids = jnp.arange(num_reqs, dtype=jnp.int32)
    req_of_tok = jnp.sum((tok_ids[:, None] >= req_ends[None, :]).astype(jnp.int32), axis=1)
    req_onehot = req_of_tok[:, None] == req_ids[None, :]
    positions = (
        jnp.sum(jnp.where(req_onehot, (prior_offsets - req_starts)[None, :], 0), axis=1) + tok_ids
    )
    mask = (
        (req_of_tok[:, None] == req_of_tok[None, :]) & (tok_ids[None, :] <= tok_ids[:, None])
    ).astype(F32)
    half = HEAD_DIM // 2
    inv_freq = jnp.power(F32(ROPE_BASE), -(2.0 * jnp.arange(half, dtype=F32)) / HEAD_DIM)
    angle = positions.astype(F32)[:, None] * inv_freq[None, :]
    cos, sin = jnp.cos(angle), jnp.sin(angle)
    cosf = jnp.concatenate([cos, cos], axis=1)
    sinf = jnp.concatenate([-sin, sin], axis=1)

    mine = jnp.arange(layers, dtype=jnp.int32) * SUBS + sub
    chosen = owners[None, :] == mine[:, None]
    start = jnp.sum(jnp.where(chosen, req_starts[None, :], 0), axis=1)
    count = jnp.sum(jnp.where(chosen, lengths[None, :], 0), axis=1)
    slots = jnp.arange(cap_pad, dtype=jnp.int32)
    pick = (
        (tok_ids[None, None, :] == start[:, None, None] + slots[None, :, None])
        & (slots[None, :, None] < count[:, None, None])
    ).astype(BF16)

    gain = lax.dynamic_index_in_dim(norm_gain, layer, 0, keepdims=False).astype(F32)
    gain = gain.reshape(pieces * chunks, 1, BLOCK)
    hin = hidden_t.reshape(SUBS, chunks, BLOCK, tokens).transpose(0, 1, 3, 2)

    vm = pltpu.VMEM
    dma = pltpu.SemaphoreType.DMA
    others = tps - 1
    far_subs = SUBS - 1
    blk = (tokens, BLOCK)
    fin, kv = pl.pallas_call(
        functools.partial(relay_kernel, layers, tps, own_tokens),
        out_shape=(
            jax.ShapeDtypeStruct((SUBS, chunks, tok_pad, BLOCK), BF16),
            jax.ShapeDtypeStruct((layers, cap_pad, 2 * HEAD_DIM), BF16),
        ),
        in_specs=[pl.BlockSpec(memory_space=pltpu.VMEM)] * 10,
        out_specs=(pl.BlockSpec(memory_space=pltpu.VMEM),) * 2,
        scratch_shapes=[
            vm((pieces, chunks) + blk, BF16),
            vm((tokens, q_cols), F32),
            vm((tokens, 2 * HEAD_DIM), F32),
            vm((tokens, HEAD_DIM), F32),
            vm((tokens, 2 * HEAD_DIM), BF16),
            vm((far_subs, tokens, 2 * HEAD_DIM), BF16),
            vm((tokens, 2 * HEAD_DIM), BF16),
            vm((tokens, q_cols), BF16),
            vm((SUBS, chunks, others) + blk, BF16),
            vm((SUBS, chunks, others) + blk, BF16),
            vm((SUBS, chunks) + blk, BF16),
            vm((far_subs, chunks) + blk, BF16),
            vm((chunks,) + blk, BF16),
            vm((tokens + 32, BLOCK), F32),
            vm((sections, chunks, tok_pad, BLOCK), BF16),
            vm((SUBS, chunks, tok_pad, BLOCK), BF16),
            vm((layers, cap_pad, 2 * HEAD_DIM), BF16),
            vm((layers, cap_pad, 2 * HEAD_DIM), BF16),
            dma((pieces, chunks)),
            dma((SUBS, chunks, others)),
            dma((far_subs, chunks)),
            dma((far_subs,)),
            dma((far_subs,)),
            dma((SUBS, chunks, others)),
            dma((SUBS, chunks, others)),
            dma((far_subs, chunks)),
            dma((far_subs, chunks)),
            dma((chunks,)),
            dma((layers,)),
            dma((layers,)),
            dma((sections,)),
            dma((SUBS,)),
        ],
        compiler_params=pltpu.CompilerParams(
            collective_id=0, has_side_effects=True, vmem_limit_bytes=56 * 1024 * 1024
        ),
        name="relay",
    )(hin, gain, q_weight[0], k_weight[0], v_weight[0], o_weight[0], cosf, sinf, mask, pick)
    final_hidden = fin[:, :, :own_tokens].transpose(0, 1, 3, 2).reshape(rows_dev, own_tokens)
    return final_hidden, kv[None, :, :capacity]


def solution(mesh):
    return jax.shard_map(
        shards,
        mesh=mesh,
        in_specs=(
            P("tp", None),
            P(),
            P("section", None, "tp"),
            P("section", None, "tp"),
            P("section", None, "tp"),
            P("section", "tp", None),
            P(),
            P(),
            P(),
        ),
        out_specs=(P("tp", "section"), P("section", None, None, "tp")),
        check_vma=False,
    )
```

time: 1440 us -> 291 us (0.20)
  waiting for transfers between devices: 1270 us -> 0 us
  Pallas kernels: 0 us -> 272 us
  other arithmetic: 76 us -> 6.1 us
  starting transfers between devices: 22 us -> 0 us
  local copies, waits for them, and re-layouts: 28.6 us -> 8.8 us
  matrix products: 14.9 us -> 0 us
  between operations: 15.6 us -> 0.72 us
    ppermute x20 -> x0, waiting for transfers between devices: 876 us -> none  [the longest x16 598 us: partner_2(): lax.ppermute(shard, axis, [(i, i ^ 1 << distance) for i in range(lax.axis...]
    pallas_call x0 -> x1, Pallas kernels: none -> 272 us  [shards(): pl.pallas_call(functools.partial(relay_kernel, layers, tps, own_tokens),...]
    reduce_scatter x5 -> x0, waiting for transfers between devices: 263 us -> none  [the longest x4 134 us: run_layer(): lax.psum_scatter(lax.cond(active, full_term, empty_term, w_out).astype(jn...]
    all_gather x5 -> x0, waiting for transfers between devices: 135 us -> none  [the longest x4 72.7 us: run_layer(): whole = lax.all_gather(piece_in, 'tp', axis=0, tiled=True)]
    select_n x11 -> x0, other arithmetic: 37.4 us -> none  [the longest x4 29.4 us: step_fn(): jnp.where(active & (layer_idx == layer_count - 1), updated, final_buf)]
    convert_element_type x21 -> x4, other arithmetic: 29.2 us -> 2.36 us  [the longest x1 0.93 us: shards(): mask = ((req_of_tok[:, None] == req_of_tok[None, :]) & (tok_ids[None, :]...]
    ppermute x20 -> x0, starting transfers between devices: 21.8 us -> none  [the longest x16 16.7 us: partner_2(): lax.ppermute(shard, axis, [(i, i ^ 1 << distance) for i in range(lax.axis...]
    dot_general x6 -> x0, matrix products: 14.9 us -> none  [the longest x1 7.23 us: full_term(): lax.dot_general(cols_now, attended, (((0,), (1,)), ((), ())), preferred_e...]
  transfers between devices with their start and end apart: 30 -> 0, of which waited for: 30 -> 0; matrix products, arithmetic and copies ran while one was open for 1% -> 0% of each run, Pallas kernels for 0% -> 0%
where the time goes in v1:
time: 291 us; the launch traced here: 288 us
  Pallas kernels  272 us (93%)
  local copies, waits for them, and re-layouts  8.8 us (3%)
  other arithmetic  6.1 us (2%)
    pallas_call x1, Pallas kernels, shards(): pl.pallas_call(functools.partial(relay_kernel, layers, tps, own_tokens),...  272 us

profile of v1, /device:TPU:28, one launch (start us, length us, event | category | flops | bytes accessed | tf_op | source)
XLA Modules:
  0.0 287.6 jit_solution(2349128681247186435)
XLA Ops:
  0.6 0.0 copy-start
  0.7 0.7 copy.16
  1.5 0.1 reduce
  1.6 0.7 fusion.7
  2.3 0.9 fusion.6
  3.1 0.1 iota_compare_fusion.4
  3.2 0.1 convert_reduce_fusion
  3.3 0.1 select_reduce_fusion
  3.4 0.1 iota_add_fusion
  3.5 0.0 copy-done
  3.5 0.6 convert.1.gain
  4.2 0.8 fusion.3.pick
  5.0 0.8 fusion.4
  5.7 0.9 pad_maximum_fusion
  6.7 0.9 fusion.1.mask
  7.6 4.6 %copy.15 = bf16[4,4,256,384]{2,3,1,0:T(8,128)(2,1)} copy(bf16[4,4,256,384]{3,2,1,0:T(8,128)(2,1)} %bitcast.17) | data formatting | bytes 6291456 | tf_op jit(solution)/shard_map/reshape | solution.py:418
  12.2 272.0 %relay.1 = (bf16[4,4,32,256]{3,2,1,0:T(8,128)(2,1)}, bf16[4,48,256]{2,1,0:T(8,128)(2,1)}) custom-call(bf16[4,4,384,256]{3,2,1,0:T(8,128)(2,1)} %bitcast.14, f32[32,1,256]{2,1,0:T(1,128)} %convert.1.gain, bf16[8192,256]{1,0:T(8,128)(2,1)} %bitcast.15, bf16[2048,128]{1,0:T(8,128)(2,1)} %bitcast.18, bf16[2048,128]{1,0:T(8,128)(2,1)} %bitcast.19, ...), custom_call_target="tpu_custom_call" | custom-call | tf_op jit(solution)/shard_map/relay/pallas_call | solution.py:425
  284.2 0.9 slice_bitcast_fusion
  285.2 0.1 copy.17
  285.2 0.8 reshape.124
  286.1 1.5 copy.19
  (5 shorter events, 0.1 us)
Async XLA Ops:
  0.6 2.8 copy-start

commit v2 on v1

v2 whole, which is shorter than its diff:
```python
import functools
import math

import jax
import jax.numpy as jnp
from jax import lax
from jax.experimental import pallas as pl
from jax.experimental.pallas import tpu as pltpu
from jax.sharding import PartitionSpec as P

HEAD_DIM = 128
SUBS = 4
BLOCK = 256
GROUP = 2
SPLIT = 4
NORM_EPS = 1e-05
ROPE_BASE = 500000.0
MESH = pl.DeviceIdType.MESH
F32 = jnp.float32
BF16 = jnp.bfloat16


def dot(a, b):
    return jnp.dot(a, b, preferred_element_type=F32)


def round_up(count, unit):
    return (count + unit - 1) // unit * unit


def relay_kernel(
    layers, tps, own_tokens,
    hin, gain, wq, wk, wv, wo, cosf, sinf, mask, pick,
    fin_out, kv_out,
    hbuf, qacc, kvacc, sumsq, kvst, kvrecv, kvb, att,
    s1out, s1in, s1own, s2in, upd, totf, fst, fin, pickst, kvbuf,
    hs, fwd_s, ag_s, kvp_s, kvp_r, s1_s, s1_r, s2_s, s2_r, z_s, pk_s, pk_r, fin_s, fin_r,
):
    section = lax.axis_index("section")
    t = lax.axis_index("tp")
    layer = section // SUBS
    u = section % SUBS
    splits, pieces, chunks, span, block = hbuf.shape
    depth = pieces * chunks * block
    group = min(GROUP, chunks)
    per_split = layers * SUBS // splits
    own = u * tps + t
    sections = layers * SUBS
    last = layers - 1
    out_tp = own // SUBS
    out_slot = own % SUBS
    base = layer * SUBS

    def copy(src, dst, send, recv, sec, core):
        return pltpu.make_async_remote_copy(
            src_ref=src, dst_ref=dst, send_sem=send, recv_sem=recv,
            device_id=(sec, core), device_id_type=MESH,
        )

    def sub_at(r):
        return (u + r) % SUBS

    def tp_at(e):
        return (t + e) % tps

    def first_copy(i, j, ci, e):
        p = t * SUBS + j
        return copy(hbuf.at[i, p, ci], hbuf.at[i, p, ci], fwd_s.at[i, j, ci, e - 1], hs.at[i, p, ci],
                    section, tp_at(e))

    def fwd_copy(i, r, ci, e):
        p = sub_at(r) * tps + t
        return copy(hbuf.at[i, p, ci], hbuf.at[i, p, ci], fwd_s.at[i, r, ci, e - 1], hs.at[i, p, ci],
                    section, tp_at(e))

    def ag_copy(i, r, ci):
        return copy(hbuf.at[i, own, ci], hbuf.at[i, own, ci], ag_s.at[i, r - 1, ci], hs.at[i, own, ci],
                    base + sub_at(r), t)

    def wait_block(i, p, ci):
        copy(hbuf.at[i, p, ci], hbuf.at[i, p, ci], fwd_s.at[0, 0, 0, 0], hs.at[i, p, ci],
             section, tp_at(1)).wait_recv()

    def kvp_copy(i, r):
        return copy(kvst.at[i], kvrecv.at[i, r - 1], kvp_s.at[i, r - 1], kvp_r.at[i, r - 1],
                    base + sub_at(r), t)

    def s1_copy(i, r, ci, e):
        return copy(s1out.at[i, r, ci, e - 1], s1in.at[i, r, ci, e - 1], s1_s.at[i, r, ci, e - 1],
                    s1_r.at[i, r, ci, e - 1], section, tp_at(e))

    def s2_copy(i, r, ci):
        return copy(s1own.at[i, r, ci], s2in.at[i, r - 1, ci], s2_s.at[i, r - 1, ci], s2_r.at[i, r - 1, ci],
                    base + sub_at(r), t)

    def z_copy(i, ci):
        return copy(upd.at[i, ci], hbuf.at[i, own, ci], z_s.at[i, ci], hs.at[i, own, ci], section + SUBS, t)

    def pick_copy(j):
        return copy(pickst.at[j], kvbuf.at[layer], pk_s.at[j], pk_r.at[layer], j * SUBS + u, t)

    def fin_copy(s):
        return copy(fst.at[s], fin.at[out_slot], fin_s.at[s], fin_r.at[out_slot], s, out_tp)

    def loop(count, body):
        def step(k, carry):
            body(k)
            return carry
        lax.fori_loop(0, count, step, jnp.int32(0))

    barrier = pltpu.get_barrier_semaphore()

    def greet(sec, core):
        pl.semaphore_signal(barrier, inc=1, device_id=(sec, core), device_id_type=MESH)

    for e in range(1, tps):
        greet(section, tp_at(e))
    for r in range(1, SUBS):
        greet(base + sub_at(r), t)
    for j in range(1, layers):
        greet((layer + j) % layers * SUBS + u, t)
    for j in range(SUBS):
        p = t * SUBS + j
        sec, core = last * SUBS + p // tps, p % tps

        @pl.when((sec != section) | (core != t))
        def _():
            greet(sec, core)

    spread_to = jnp.where(layer == last, sections - jnp.where(out_tp == t, 1, 0), 0)
    pl.semaphore_wait(barrier, (tps - 1) + (SUBS - 1) + (layers - 1) + spread_to)

    totf[...] = jnp.zeros_like(totf)
    kvb[0] = jnp.zeros_like(kvb[0])

    @pl.when(layer == 0)
    def _():
        def send(k):
            j, ci = k // chunks, k % chunks
            rows = pl.ds(pl.multiple_of(k * block, block), block)
            turned = hin[rows, :].astype(F32).T.astype(BF16)
            for i in range(splits):
                hbuf[i, t * SUBS + j, ci] = turned[i * span:(i + 1) * span]
                for e in range(1, tps):
                    first_copy(i, j, ci, e).start()
        loop(SUBS * chunks, send)

    def spread(i, ci):
        wait_block(i, own, ci)
        for r in range(1, SUBS):
            ag_copy(i, r, ci).start()
        for e in range(1, tps):
            fwd_copy(i, 0, ci, e).start()

    def rotate(x, i):
        return x * cosf[i] + pltpu.roll(x, HEAD_DIM // 2, 1) * sinf[i]

    def stage(i):
        qacc[...] = jnp.zeros_like(qacc)
        kvacc[...] = jnp.zeros_like(kvacc)
        sumsq[...] = jnp.zeros_like(sumsq)

        @pl.when(layer == 0)
        def _():
            def arrive(k):
                j, ci = k // chunks, k % chunks
                for e in range(1, tps):
                    wait_block(i, tp_at(e) * SUBS + j, ci)
            loop(SUBS * chunks, arrive)

        @pl.when((layer > 0) & (i == 0))
        def _():
            loop(chunks, lambda ci: spread(0, ci))

        def absorb(p, n):
            parts, squares = [], 0.0
            for m in range(group):
                ci = n * group + m
                x = hbuf[i, p, ci].astype(F32)
                sq = x * x
                for w in range(block // HEAD_DIM):
                    squares = squares + sq[:, w * HEAD_DIM:(w + 1) * HEAD_DIM]
                parts.append((x * gain[p * chunks + ci]).astype(BF16))
            scaled = jnp.concatenate(parts, axis=1)
            width = group * block
            rows = pl.ds(pl.multiple_of(p * chunks * block + n * width, width), width)
            return scaled, dot(scaled, wq[rows, :]), squares

        def near(n):
            for m in range(group):
                for e in range(1, tps):
                    @pl.when(layer > 0)
                    def _():
                        wait_block(i, u * tps + tp_at(e), n * group + m)
            query_sum, square_sum, kv_sum = 0.0, 0.0, 0.0
            width = group * block
            for e in range(tps):
                d = tp_at(e)
                scaled, query, squares = absorb(u * tps + d, n)
                query_sum, square_sum = query_sum + query, square_sum + squares
                rows = pl.ds(pl.multiple_of(d * chunks * block + n * width, width), width)
                kv_sum = kv_sum + dot(scaled, jnp.concatenate([wk[rows, :], wv[rows, :]], axis=1))
            qacc[...] += query_sum
            sumsq[...] += square_sum
            kvacc[...] += kv_sum
        loop(chunks // group, near)

        kvst[i] = kvacc[...].astype(BF16)
        for r in range(1, SUBS):
            kvp_copy(i, r).start()

        def take(n, core):
            query_sum, square_sum = 0.0, 0.0
            for r in range(1, SUBS):
                scaled, query, squares = absorb(sub_at(r) * tps + core, n)
                query_sum, square_sum = query_sum + query, square_sum + squares
            qacc[...] += query_sum
            sumsq[...] += square_sum

        def across(n):
            @pl.when(layer > 0)
            def _():
                for m in range(group):
                    for r in range(1, SUBS):
                        ci = n * group + m
                        wait_block(i, sub_at(r) * tps + t, ci)
                        for e in range(1, tps):
                            fwd_copy(i, r, ci, e).start()
            take(n, t)
        loop(chunks // group, across)

        def far(n):
            for e in range(1, tps):
                @pl.when(layer > 0)
                def _():
                    for m in range(group):
                        for r in range(1, SUBS):
                            wait_block(i, sub_at(r) * tps + tp_at(e), n * group + m)
                take(n, tp_at(e))
        loop(chunks // group, far)

        scale = lax.rsqrt(jnp.sum(sumsq[...], axis=1, keepdims=True) / depth + NORM_EPS)
        kv = kvacc[...]
        for r in range(1, SUBS):
            kvp_copy(i, r).wait_recv()
            kv = kv + kvrecv[i, r - 1].astype(F32)
        kv = kv * scale
        kvb[i + 1, :, :HEAD_DIM] = rotate(kv[:, :HEAD_DIM], i).astype(BF16)
        kvb[i + 1, :, HEAD_DIM:] = kv[:, HEAD_DIM:].astype(BF16)
        both = jnp.concatenate([kvb[i], kvb[i + 1]], axis=0)
        for g in range(att.shape[1] // HEAD_DIM):
            cols = slice(g * HEAD_DIM, (g + 1) * HEAD_DIM)
            query = rotate(qacc[:, cols] * scale, i).astype(BF16)
            scores = lax.dot_general(
                query, both[:, :HEAD_DIM], (((1,), (1,)), ((), ())), preferred_element_type=F32
            ) * (1.0 / math.sqrt(HEAD_DIM))
            weights = jnp.where(mask[i] > 0.0, jnp.exp(scores), 0.0)
            probs = (weights / jnp.sum(weights, axis=1, keepdims=True)).astype(BF16)
            att[:, cols] = dot(probs, both[:, HEAD_DIM:]).astype(BF16)

        def term(p, ci):
            cols = pl.ds(pl.multiple_of((p * chunks + ci) * block, block), block)
            return dot(att[...], wo[:, cols]).astype(BF16)

        def project(k):
            @pl.when(k < chunks)
            def _():
                for e in range(1, tps):
                    for r in (1, 2, 3, 0):
                        s1out[i, r, k, e - 1] = term(sub_at(r) * tps + tp_at(e), k)
                    for r in (1, 2, 3, 0):
                        s1_copy(i, r, k, e).start()
                for r in range(SUBS):
                    s1own[i, r, k] = term(sub_at(r) * tps + t, k)

            @pl.when(k >= 1)
            def _():
                ci = k - 1
                for r in (1, 2, 3, 0):
                    total = s1own[i, r, ci].astype(F32)
                    for e in range(1, tps):
                        s1_copy(i, r, ci, e).wait_recv()
                        total = total + s1in[i, r, ci, e - 1].astype(F32)
                    s1own[i, r, ci] = total.astype(BF16)
                    if r > 0:
                        s2_copy(i, r, ci).start()
        loop(chunks + 1, project)

        @pl.when(i == splits - 1)
        def _():
            def deliver(j):
                rows = dot(pick[j, 0], kvb[1])
                for n in range(1, splits):
                    rows = rows + dot(pick[j, n], kvb[n + 1])
                pickst[j] = rows.astype(BF16)

                @pl.when(j == layer)
                def _():
                    kvbuf[layer] = pickst[j]

                @pl.when(j != layer)
                def _():
                    pick_copy(j).start()
            loop(layers, deliver)

        def finish(ci):
            @pl.when(ci < chunks)
            def _():
                terms = s1own[i, 0, ci].astype(F32)
                for r in range(1, SUBS):
                    s2_copy(i, r, ci).wait_recv()
                    terms = terms + s2in[i, r - 1, ci].astype(F32)
                total = hbuf[i, own, ci].astype(F32) + terms

                @pl.when(layer < last)
                def _():
                    upd[i, ci] = total.astype(BF16)
                    z_copy(i, ci).start()

                @pl.when(layer == last)
                def _():
                    totf[:span] = total
                    for n in range(per_split):
                        rows = totf[n * own_tokens:n * own_tokens + fst.shape[2]]
                        fst[i * per_split + n, ci] = rows.astype(BF16)

            @pl.when((ci >= 1) & (layer > 0) & (i < splits - 1))
            def _():
                spread(i + 1, ci - 1)
        loop(chunks + 1, finish)

        @pl.when(layer == last)
        def _():
            def out(n):
                s = i * per_split + n
                mine = (s == section) & (out_tp == t)

                @pl.when(mine)
                def _():
                    fin[out_slot] = fst[s]

                @pl.when(jnp.logical_not(mine))
                def _():
                    fin_copy(s).start()
            loop(per_split, out)

    loop(splits, stage)

    def kv_in(j):
        @pl.when(j != layer)
        def _():
            copy(pickst.at[j], kvbuf.at[j], pk_s.at[j], pk_r.at[j], j * SUBS + u, t).wait_recv()
    loop(layers, kv_in)
    kv_out[...] = kvbuf[...]

    def fin_in(j):
        p = t * SUBS + j
        sec, core = last * SUBS + p // tps, p % tps

        @pl.when((sec != section) | (core != t))
        def _():
            copy(fst.at[0], fin.at[j], fin_s.at[0], fin_r.at[j], sec, core).wait_recv()
    loop(SUBS, fin_in)
    fin_out[...] = fin[...]

    @pl.when(layer == 0)
    def _():
        def sent(k):
            for e in range(1, tps):
                first_copy(k // (SUBS * chunks), k // chunks % SUBS, k % chunks, e).wait_send()
        loop(splits * SUBS * chunks, sent)

    @pl.when(layer > 0)
    def _():
        def sent(k):
            i, ci = k // chunks, k % chunks
            for r in range(SUBS):
                for e in range(1, tps):
                    fwd_copy(i, r, ci, e).wait_send()
            for r in range(1, SUBS):
                ag_copy(i, r, ci).wait_send()
        loop(splits * chunks, sent)

    def kvp_sent(i):
        for r in range(1, SUBS):
            kvp_copy(i, r).wait_send()
    loop(splits, kvp_sent)

    def sums_sent(k):
        i, ci = k // chunks, k % chunks
        for r in range(SUBS):
            for e in range(1, tps):
                s1_copy(i, r, ci, e).wait_send()
        for r in range(1, SUBS):
            s2_copy(i, r, ci).wait_send()

        @pl.when(layer < last)
        def _():
            z_copy(i, ci).wait_send()
    loop(splits * chunks, sums_sent)

    def kv_sent(j):
        @pl.when(j != layer)
        def _():
            pick_copy(j).wait_send()
    loop(layers, kv_sent)

    @pl.when(layer == last)
    def _():
        def sent(s):
            @pl.when(jnp.logical_not((s == section) & (out_tp == t)))
            def _():
                fin_copy(s).wait_send()
        loop(sections, sent)


def shards(
    hidden_t, norm_gain, q_weight, k_weight, v_weight, o_weight, lengths, prior_offsets, owners
):
    sections = lax.axis_size("section")
    tps = lax.axis_size("tp")
    section = lax.axis_index("section")
    layers = sections // SUBS
    layer = section // SUBS
    sub = section % SUBS
    rows_dev, tokens = hidden_t.shape
    num_reqs = lengths.shape[0]
    capacity = 2 * tokens // num_reqs
    cap_pad = round_up(capacity, 16)
    own_tokens = tokens // sections
    tok_pad = round_up(own_tokens, 16)
    pieces = SUBS * tps
    block = min(BLOCK, rows_dev // SUBS)
    chunks = rows_dev // SUBS // block
    q_cols = q_weight.shape[2]
    span = tokens // SPLIT
    assert span >= capacity and sections % SPLIT == 0 and span % 16 == 0

    req_ends = jnp.cumsum(lengths)
    req_starts = req_ends - lengths
    tok_ids = jnp.arange(tokens, dtype=jnp.int32)
    req_ids = jnp.arange(num_reqs, dtype=jnp.int32)
    req_of_tok = jnp.sum((tok_ids[:, None] >= req_ends[None, :]).astype(jnp.int32), axis=1)
    req_onehot = req_of_tok[:, None] == req_ids[None, :]
    positions = (
        jnp.sum(jnp.where(req_onehot, (prior_offsets - req_starts)[None, :], 0), axis=1) + tok_ids
    )
    spans = jnp.arange(SPLIT, dtype=jnp.int32)[:, None, None] * span
    query_ids = spans + jnp.arange(span, dtype=jnp.int32)[None, :, None]
    key_ids = spans + jnp.arange(-span, span, dtype=jnp.int32)[None, None, :]
    first_ids = jnp.sum(jnp.where(req_onehot, req_starts[None, :], 0), axis=1).reshape(SPLIT, span, 1)
    mask = ((key_ids >= first_ids) & (key_ids <= query_ids)).astype(F32)
    half = HEAD_DIM // 2
    inv_freq = jnp.power(F32(ROPE_BASE), -(2.0 * jnp.arange(half, dtype=F32)) / HEAD_DIM)
    angle = positions.astype(F32)[:, None] * inv_freq[None, :]
    cos, sin = jnp.cos(angle), jnp.sin(angle)
    cosf = jnp.concatenate([cos, cos], axis=1).reshape(SPLIT, span, HEAD_DIM)
    sinf = jnp.concatenate([-sin, sin], axis=1).reshape(SPLIT, span, HEAD_DIM)

    mine = jnp.arange(layers, dtype=jnp.int32) * SUBS + sub
    chosen = owners[None, :] == mine[:, None]
    start = jnp.sum(jnp.where(chosen, req_starts[None, :], 0), axis=1)
    count = jnp.sum(jnp.where(chosen, lengths[None, :], 0), axis=1)
    slots = jnp.arange(cap_pad, dtype=jnp.int32)
    tok_split = tok_ids.reshape(1, SPLIT, 1, span)
    slots = slots[None, None, :, None]
    pick = (
        (tok_split == start[:, None, None, None] + slots) & (slots < count[:, None, None, None])
    ).astype(BF16)

    gain = lax.dynamic_index_in_dim(norm_gain, layer, 0, keepdims=False).astype(F32)
    gain = gain.reshape(pieces * chunks, 1, block)

    vm = pltpu.VMEM
    dma = pltpu.SemaphoreType.DMA
    others = tps - 1
    far_subs = SUBS - 1
    blk = (span, block)
    kv_cols = 2 * HEAD_DIM
    fin, kv = pl.pallas_call(
        functools.partial(relay_kernel, layers, tps, own_tokens),
        out_shape=(
            jax.ShapeDtypeStruct((SUBS, chunks, tok_pad, block), BF16),
            jax.ShapeDtypeStruct((layers, cap_pad, 2 * HEAD_DIM), BF16),
        ),
        in_specs=[pl.BlockSpec(memory_space=pltpu.VMEM)] * 10,
        out_specs=(pl.BlockSpec(memory_space=pltpu.VMEM),) * 2,
        scratch_shapes=[
            vm((SPLIT, pieces, chunks) + blk, BF16),
            vm((span, q_cols), F32),
            vm((span, kv_cols), F32),
            vm((span, HEAD_DIM), F32),
            vm((SPLIT, span, kv_cols), BF16),
            vm((SPLIT, far_subs, span, kv_cols), BF16),
            vm((SPLIT + 1, span, kv_cols), BF16),
            vm((span, q_cols), BF16),
            vm((SPLIT, SUBS, chunks, others) + blk, BF16),
            vm((SPLIT, SUBS, chunks, others) + blk, BF16),
            vm((SPLIT, SUBS, chunks) + blk, BF16),
            vm((SPLIT, far_subs, chunks) + blk, BF16),
            vm((SPLIT, chunks) + blk, BF16),
            vm((span + 32, block), F32),
            vm((sections, chunks, tok_pad, block), BF16),
            vm((SUBS, chunks, tok_pad, block), BF16),
            vm((layers, cap_pad, 2 * HEAD_DIM), BF16),
            vm((layers, cap_pad, 2 * HEAD_DIM), BF16),
            dma((SPLIT, pieces, chunks)),
            dma((SPLIT, SUBS, chunks, others)),
            dma((SPLIT, far_subs, chunks)),
            dma((SPLIT, far_subs)),
            dma((SPLIT, far_subs)),
            dma((SPLIT, SUBS, chunks, others)),
            dma((SPLIT, SUBS, chunks, others)),
            dma((SPLIT, far_subs, chunks)),
            dma((SPLIT, far_subs, chunks)),
            dma((SPLIT, chunks)),
            dma((layers,)),
            dma((layers,)),
            dma((sections,)),
            dma((SUBS,)),
        ],
        compiler_params=pltpu.CompilerParams(
            collective_id=0, has_side_effects=True, vmem_limit_bytes=56 * 1024 * 1024
        ),
        name="relay",
    )(hidden_t, gain, q_weight[0], k_weight[0], v_weight[0], o_weight[0], cosf, sinf, mask, pick)
    final_hidden = fin[:, :, :own_tokens].transpose(0, 1, 3, 2).reshape(rows_dev, own_tokens)
    return final_hidden, kv[None, :, :capacity]


def solution(mesh):
    return jax.shard_map(
        shards,
        mesh=mesh,
        in_specs=(
            P("tp", None),
            P(),
            P("section", None, "tp"),
            P("section", None, "tp"),
            P("section", None, "tp"),
            P("section", "tp", None),
            P(),
            P(),
            P(),
        ),
        out_specs=(P("tp", "section"), P("section", None, None, "tp")),
        check_vma=False,
    )
```

time: 291 us -> 189 us (0.65); the launches traced: 288 us -> 189 us
  Pallas kernels: 272 us -> 178 us
  local copies, waits for them, and re-layouts: 8.8 us -> 4.32 us
    pallas_call x1, Pallas kernels: 272 us -> 178 us  [shards(): pl.pallas_call(functools.partial(relay_kernel, layers, tps, own_tokens),...]
    reshape x1 -> x0, local copies, waits for them, and re-layouts: 4.64 us -> none  [shards(): hin = hidden_t.reshape(SUBS, chunks, BLOCK, tokens).transpose(0, 1, 3, 2)]
where the time goes in v2:
time: 189 us
  Pallas kernels  178 us (94%)
  other arithmetic  6.28 us (3%)
  local copies, waits for them, and re-layouts  4.32 us (2%)
    pallas_call x1, Pallas kernels, shards(): pl.pallas_call(functools.partial(relay_kernel, layers, tps, own_tokens),...  178 us

profile of v2, /device:TPU:28, one launch (start us, length us, event | category | flops | bytes accessed | tf_op | source)
XLA Modules:
  0.0 188.8 jit_solution(10892479485441355673)
XLA Ops:
  0.6 0.0 copy-start
  0.7 0.7 copy.14
  1.4 0.1 reduce
  1.6 0.7 fusion.3
  2.2 0.9 fusion.2
  3.1 0.1 iota_add_fusion
  3.2 0.1 iota_compare_fusion.2
  3.3 0.8 and_convert_fusion.pick
  4.1 0.0 copy-done
  4.1 0.6 convert.1.gain
  4.8 0.1 convert_reduce_fusion
  4.9 0.1 select_reduce_fusion
  5.0 0.1 reduce_sum.49
  5.1 0.8 fusion
  5.9 0.9 pad_maximum_fusion
  6.8 0.1 ge.34
  6.9 0.1 broadcast_add_fusion
  6.9 0.1 iota_add_fusion.1
  7.0 0.9 and_convert_fusion.1.mask
  7.9 177.5 %relay.1 = (bf16[4,4,32,256]{3,2,1,0:T(8,128)(2,1)}, bf16[4,48,256]{2,1,0:T(8,128)(2,1)}) custom-call(bf16[4096,384]{1,0:T(8,128)(2,1)} %hin.1, f32[32,1,256]{2,1,0:T(1,128)} %convert.1.gain, bf16[8192,256]{1,0:T(8,128)(2,1)} %bitcast.12, bf16[2048,128]{1,0:T(8,128)(2,1)} %bitcast.14, bf16[2048,128]{1,0:T(8,128)(2,1)} %bitcast.15, ...), custom_call_target="tpu_custom_call" | custom-call | tf_op jit(solution)/shard_map/relay/pallas_call | solution.py:480
  185.4 0.9 slice_bitcast_fusion
  186.4 0.1 copy.15
  186.5 0.8 reshape.243
  187.3 1.5 copy.17
  (8 shorter events, 0.1 us)
Async XLA Ops:
  0.6 3.5 %copy-start = (bf16[4,8192]{1,0:T(4,128)(2,1)S(1)}, bf16[4,8192]{1,0:T(4,128)(2,1)}, u32[]{:S(2)}) copy-start(bf16[4,8192]{1,0:T(4,128)(2,1)} %param.10) | copy-start | bytes 196612

commit v3 on v2

--- a/solution.py
+++ b/solution.py
@@ -57,8 +57,15 @@
             device_id=(sec, core), device_id_type=MESH,
         )
 
+    along_x = u + 1 - 2 * (u % 2)
+    along_y = (u + 2) % SUBS
+    subs = (u, along_x, along_y, (along_x + 2) % SUBS)
+
     def sub_at(r):
-        return (u + r) % SUBS
+        return subs[r]
+
+    def side(which):
+        return along_x + (along_y - along_x) * which
 
     def tp_at(e):
         return (t + e) % tps
@@ -77,6 +84,11 @@
         return copy(hbuf.at[i, own, ci], hbuf.at[i, own, ci], ag_s.at[i, r - 1, ci], hs.at[i, own, ci],
                     base + sub_at(r), t)
 
+    def hop_copy(i, ci):
+        p = side(ci % 2) * tps + t
+        return copy(hbuf.at[i, p, ci], hbuf.at[i, p, ci], ag_s.at[i, 2, ci], hs.at[i, p, ci],
+                    base + side(1 - ci % 2), t)
+
     def wait_block(i, p, ci):
         copy(hbuf.at[i, p, ci], hbuf.at[i, p, ci], fwd_s.at[0, 0, 0, 0], hs.at[i, p, ci],
              section, tp_at(1)).wait_recv()
@@ -89,9 +101,13 @@
         return copy(s1out.at[i, r, ci, e - 1], s1in.at[i, r, ci, e - 1], s1_s.at[i, r, ci, e - 1],
                     s1_r.at[i, r, ci, e - 1], section, tp_at(e))
 
-    def s2_copy(i, r, ci):
-        return copy(s1own.at[i, r, ci], s2in.at[i, r - 1, ci], s2_s.at[i, r - 1, ci], s2_r.at[i, r - 1, ci],
-                    base + sub_at(r), t)
+    def s2_copy(i, which, ci):
+        return copy(s1own.at[i, which + 1, ci], s2in.at[i, which, ci], s2_s.at[i, which, ci],
+                    s2_r.at[i, which, ci], base + side(which), t)
+
+    def cross_copy(i, ci):
+        return copy(s1own.at[i, 3, ci], s2in.at[i, 2, ci], s2_s.at[i, 2, ci], s2_r.at[i, 2, ci],
+                    base + side(ci % 2), t)
 
     def z_copy(i, ci):
         return copy(upd.at[i, ci], hbuf.at[i, own, ci], z_s.at[i, ci], hs.at[i, own, ci], section + SUBS, t)
@@ -147,7 +163,7 @@
 
     def spread(i, ci):
         wait_block(i, own, ci)
-        for r in range(1, SUBS):
+        for r in (1, 2):
             ag_copy(i, r, ci).start()
         for e in range(1, tps):
             fwd_copy(i, 0, ci, e).start()
@@ -209,9 +225,9 @@
         for r in range(1, SUBS):
             kvp_copy(i, r).start()
 
-        def take(n, core):
+        def take(n, core, sides):
             query_sum, square_sum = 0.0, 0.0
-            for r in range(1, SUBS):
+            for r in sides:
                 scaled, query, squares = absorb(sub_at(r) * tps + core, n)
                 query_sum, square_sum = query_sum + query, square_sum + squares
             qacc[...] += query_sum
@@ -221,23 +237,37 @@
             @pl.when(layer > 0)
             def _():
                 for m in range(group):
-                    for r in range(1, SUBS):
-                        ci = n * group + m
+                    ci = n * group + m
+                    for r in (1, 2):
                         wait_block(i, sub_at(r) * tps + t, ci)
+                    hop_copy(i, ci).start()
+                    for r in (1, 2):
                         for e in range(1, tps):
                             fwd_copy(i, r, ci, e).start()
-            take(n, t)
+            take(n, t, (1, 2))
         loop(chunks // group, across)
 
-        def far(n):
+        def far(n, sides):
             for e in range(1, tps):
                 @pl.when(layer > 0)
                 def _():
                     for m in range(group):
-                        for r in range(1, SUBS):
+                        for r in sides:
                             wait_block(i, sub_at(r) * tps + tp_at(e), n * group + m)
-                take(n, tp_at(e))
-        loop(chunks // group, far)
+                take(n, tp_at(e), sides)
+        loop(chunks // group, lambda n: far(n, (1, 2)))
+
+        def diagonal(n):
+            @pl.when(layer > 0)
+            def _():
+                for m in range(group):
+                    ci = n * group + m
+                    wait_block(i, sub_at(3) * tps + t, ci)
+                    for e in range(1, tps):
+                        fwd_copy(i, 3, ci, e).start()
+            take(n, t, (3,))
+        loop(chunks // group, diagonal)
+        loop(chunks // group, lambda n: far(n, (3,)))
 
         scale = lax.rsqrt(jnp.sum(sumsq[...], axis=1, keepdims=True) / depth + NORM_EPS)
         kv = kvacc[...]
@@ -266,25 +296,35 @@
             @pl.when(k < chunks)
             def _():
                 for e in range(1, tps):
-                    for r in (1, 2, 3, 0):
+                    for r in (3, 1, 2, 0):
                         s1out[i, r, k, e - 1] = term(sub_at(r) * tps + tp_at(e), k)
-                    for r in (1, 2, 3, 0):
+                    for r in (3, 1, 2, 0):
                         s1_copy(i, r, k, e).start()
                 for r in range(SUBS):
                     s1own[i, r, k] = term(sub_at(r) * tps + t, k)
 
-            @pl.when(k >= 1)
+            @pl.when((k >= 1) & (k <= chunks))
             def _():
                 ci = k - 1
-                for r in (1, 2, 3, 0):
+                for r in (3, 1, 2, 0):
                     total = s1own[i, r, ci].astype(F32)
                     for e in range(1, tps):
                         s1_copy(i, r, ci, e).wait_recv()
                         total = total + s1in[i, r, ci, e - 1].astype(F32)
                     s1own[i, r, ci] = total.astype(BF16)
-                    if r > 0:
-                        s2_copy(i, r, ci).start()
-        loop(chunks + 1, project)
+                    if r == 3:
+                        cross_copy(i, ci).start()
+                s2_copy(i, ci % 2, ci).start()
+
+            @pl.when(k >= 2)
+            def _():
+                ci = k - 2
+                cross_copy(i, ci).wait_recv()
+                r = 2 - ci % 2
+                passed = s1own[i, r, ci].astype(F32) + s2in[i, 2, ci].astype(F32)
+                s1own[i, r, ci] = passed.astype(BF16)
+                s2_copy(i, 1 - ci % 2, ci).start()
+        loop(chunks + 2, project)
 
         @pl.when(i == splits - 1)
         def _():
@@ -307,9 +347,9 @@
             @pl.when(ci < chunks)
             def _():
                 terms = s1own[i, 0, ci].astype(F32)
-                for r in range(1, SUBS):
-                    s2_copy(i, r, ci).wait_recv()
-                    terms = terms + s2in[i, r - 1, ci].astype(F32)
+                for which in (0, 1):
+                    s2_copy(i, which, ci).wait_recv()
+                    terms = terms + s2in[i, which, ci].astype(F32)
                 total = hbuf[i, own, ci].astype(F32) + terms
 
                 @pl.when(layer < last)
@@ -377,8 +417,9 @@
             for r in range(SUBS):
                 for e in range(1, tps):
                     fwd_copy(i, r, ci, e).wait_send()
-            for r in range(1, SUBS):
+            for r in (1, 2):
                 ag_copy(i, r, ci).wait_send()
+            hop_copy(i, ci).wait_send()
         loop(splits * chunks, sent)
 
     def kvp_sent(i):
@@ -391,8 +432,9 @@
         for r in range(SUBS):
             for e in range(1, tps):
                 s1_copy(i, r, ci, e).wait_send()
-        for r in range(1, SUBS):
-            s2_copy(i, r, ci).wait_send()
+        for which in (0, 1):
+            s2_copy(i, which, ci).wait_send()
+        cross_copy(i, ci).wait_send()
 
         @pl.when(layer < last)
         def _():

time: 189 us -> 199 us (1.053)
  Pallas kernels: 178 us -> 187 us
    pallas_call x1, Pallas kernels: 178 us -> 187 us  [shards(): pl.pallas_call(functools.partial(relay_kernel, layers, tps, own_tokens),...]
where the time goes in v3:
time: 199 us; the launch traced here: 198 us
  Pallas kernels  187 us (94%)
  other arithmetic  6.28 us (3%)
  local copies, waits for them, and re-layouts  4.32 us (2%)
    pallas_call x1, Pallas kernels, shards(): pl.pallas_call(functools.partial(relay_kernel, layers, tps, own_tokens),...  187 us

profile of v3, /device:TPU:28, one launch (start us, length us, event | category | flops | bytes accessed | tf_op | source)
XLA Modules:
  0.0 198.1 jit_solution(3637978827432884688)
XLA Ops:
  0.6 0.0 copy-start
  0.7 0.7 copy.14
  1.4 0.1 reduce
  1.6 0.7 fusion.3
  2.2 0.9 fusion.2
  3.1 0.1 iota_add_fusion
  3.2 0.1 iota_compare_fusion.2
  3.3 0.8 and_convert_fusion.pick
  4.1 0.0 copy-done
  4.1 0.6 convert.1.gain
  4.8 0.1 convert_reduce_fusion
  4.9 0.1 select_reduce_fusion
  5.0 0.1 reduce_sum.49
  5.1 0.8 fusion
  5.9 0.9 pad_maximum_fusion
  6.8 0.1 ge.34
  6.9 0.1 broadcast_add_fusion
  6.9 0.1 iota_add_fusion.1
  7.0 0.9 and_convert_fusion.1.mask
  7.9 186.8 %relay.1 = (bf16[4,4,32,256]{3,2,1,0:T(8,128)(2,1)}, bf16[4,48,256]{2,1,0:T(8,128)(2,1)}) custom-call(bf16[4096,384]{1,0:T(8,128)(2,1)} %hin.1, f32[32,1,256]{2,1,0:T(1,128)} %convert.1.gain, bf16[8192,256]{1,0:T(8,128)(2,1)} %bitcast.12, bf16[2048,128]{1,0:T(8,128)(2,1)} %bitcast.14, bf16[2048,128]{1,0:T(8,128)(2,1)} %bitcast.15, ...), custom_call_target="tpu_custom_call" | custom-call | tf_op jit(solution)/shard_map/relay/pallas_call | solution.py:522
  194.7 0.9 slice_bitcast_fusion
  195.7 0.1 copy.15
  195.8 0.8 reshape.243
  196.6 1.5 copy.17
  (8 shorter events, 0.1 us)
Async XLA Ops:
  0.6 3.5 %copy-start = (bf16[4,8192]{1,0:T(4,128)(2,1)S(1)}, bf16[4,8192]{1,0:T(4,128)(2,1)}, u32[]{:S(2)}) copy-start(bf16[4,8192]{1,0:T(4,128)(2,1)} %param.10) | copy-start | bytes 196612

commit v4 on v2

--- a/solution.py
+++ b/solution.py
@@ -10,8 +10,8 @@
 
 HEAD_DIM = 128
 SUBS = 4
-BLOCK = 256
-GROUP = 2
+BLOCK = 512
+GROUP = 1
 SPLIT = 4
 NORM_EPS = 1e-05
 ROPE_BASE = 500000.0

time: 189 us -> 203 us (1.074)
  Pallas kernels: 178 us -> 191 us
    pallas_call x1, Pallas kernels: 178 us -> 191 us  [shards(): pl.pallas_call(functools.partial(relay_kernel, layers, tps, own_tokens),...]
where the time goes in v4:
time: 203 us; the launch traced here: 202 us
  Pallas kernels  191 us (94%)
  other arithmetic  6.28 us (3%)
  local copies, waits for them, and re-layouts  4.39 us (2%)
    pallas_call x1, Pallas kernels, shards(): pl.pallas_call(functools.partial(relay_kernel, layers, tps, own_tokens),...  191 us

profile of v4, /device:TPU:28, one launch (start us, length us, event | category | flops | bytes accessed | tf_op | source)
XLA Modules:
  0.0 202.4 jit_solution(9066359005229298168)
XLA Ops:
  0.6 0.0 copy-start
  0.7 0.7 copy.14
  1.4 0.1 reduce
  1.6 0.7 fusion.3
  2.2 0.9 fusion.2
  3.1 0.1 iota_add_fusion
  3.2 0.1 iota_compare_fusion.2
  3.3 0.8 and_convert_fusion.pick
  4.1 0.0 copy-done
  4.1 0.6 convert.1.gain
  4.8 0.1 convert_reduce_fusion
  4.9 0.1 select_reduce_fusion
  5.0 0.1 reduce_sum.49
  5.1 0.8 fusion
  5.9 0.9 pad_maximum_fusion
  6.8 0.1 ge.34
  6.9 0.1 broadcast_add_fusion
  6.9 0.1 iota_add_fusion.1
  7.0 0.9 and_convert_fusion.1.mask
  7.9 191.0 %relay.1 = (bf16[4,2,32,512]{3,2,1,0:T(8,128)(2,1)}, bf16[4,48,256]{2,1,0:T(8,128)(2,1)}) custom-call(bf16[4096,384]{1,0:T(8,128)(2,1)} %hin.1, f32[16,1,512]{2,1,0:T(1,128)} %convert.1.gain, bf16[8192,256]{1,0:T(8,128)(2,1)} %bitcast.12, bf16[2048,128]{1,0:T(8,128)(2,1)} %bitcast.14, bf16[2048,128]{1,0:T(8,128)(2,1)} %bitcast.15, ...), custom_call_target="tpu_custom_call" | custom-call | tf_op jit(solution)/shard_map/relay/pallas_call | solution.py:480
  198.9 0.9 slice_bitcast_fusion
  199.9 0.2 copy.15
  200.0 0.8 reshape.243
  200.8 1.5 copy.17
  (8 shorter events, 0.1 us)
Async XLA Ops:
  0.6 3.5 %copy-start = (bf16[4,8192]{1,0:T(4,128)(2,1)S(1)}, bf16[4,8192]{1,0:T(4,128)(2,1)}, u32[]{:S(2)}) copy-start(bf16[4,8192]{1,0:T(4,128)(2,1)} %param.10) | copy-start | bytes 196612

commit v5 on v2

--- a/solution.py
+++ b/solution.py
@@ -30,11 +30,12 @@
 
 def relay_kernel(
     layers, tps, own_tokens,
-    hin, gain, wq, wk, wv, wo, cosf, sinf, mask, pick,
+    hin_hbm, wq_hbm, wk_hbm, wv_hbm, wo_hbm, gain, cosf, sinf, first, pick,
     fin_out, kv_out,
     hbuf, qacc, kvacc, sumsq, kvst, kvrecv, kvb, att,
     s1out, s1in, s1own, s2in, upd, totf, fst, fin, pickst, kvbuf,
     hs, fwd_s, ag_s, kvp_s, kvp_r, s1_s, s1_r, s2_s, s2_r, z_s, pk_s, pk_r, fin_s, fin_r,
+    hin, wq, wk, wv, wo, load_s,
 ):
     section = lax.axis_index("section")
     t = lax.axis_index("tp")
@@ -108,6 +109,20 @@
             return carry
         lax.fori_loop(0, count, step, jnp.int32(0))
 
+    def load(n, src, dst):
+        return pltpu.make_async_copy(src, dst, load_s.at[n])
+
+    in_load = load(0, hin_hbm, hin)
+    out_load = load(4, wo_hbm, wo)
+    loads = (load(1, wq_hbm, wq), load(2, wk_hbm, wk), load(3, wv_hbm, wv))
+
+    @pl.when(layer == 0)
+    def _():
+        in_load.start()
+    for each in loads:
+        each.start()
+    out_load.start()
+
     barrier = pltpu.get_barrier_semaphore()
 
     def greet(sec, core):
@@ -135,15 +150,29 @@
 
     @pl.when(layer == 0)
     def _():
+        in_load.wait()
+        wide = round_up(span, HEAD_DIM)
+
         def send(k):
             j, ci = k // chunks, k % chunks
             rows = pl.ds(pl.multiple_of(k * block, block), block)
-            turned = hin[rows, :].astype(F32).T.astype(BF16)
-            for i in range(splits):
-                hbuf[i, t * SUBS + j, ci] = turned[i * span:(i + 1) * span]
-                for e in range(1, tps):
-                    first_copy(i, j, ci, e).start()
+            turned = hin[rows, :wide].astype(F32).T.astype(BF16)
+            hbuf[0, t * SUBS + j, ci] = turned[:span]
+            for e in range(1, tps):
+                first_copy(0, j, ci, e).start()
         loop(SUBS * chunks, send)
+
+    def send_rest(k):
+        j, ci = k // chunks, k % chunks
+        rows = pl.ds(pl.multiple_of(k * block, block), block)
+        turned = hin[rows, :].astype(F32).T.astype(BF16)
+        for i in range(1, splits):
+            hbuf[i, t * SUBS + j, ci] = turned[i * span:(i + 1) * span]
+            for e in range(1, tps):
+                first_copy(i, j, ci, e).start()
+
+    for each in loads:
+        each.wait()
 
     def spread(i, ci):
         wait_block(i, own, ci)
@@ -248,15 +277,22 @@
         kvb[i + 1, :, :HEAD_DIM] = rotate(kv[:, :HEAD_DIM], i).astype(BF16)
         kvb[i + 1, :, HEAD_DIM:] = kv[:, HEAD_DIM:].astype(BF16)
         both = jnp.concatenate([kvb[i], kvb[i + 1]], axis=0)
+        key_ids = (i - 1) * span + lax.broadcasted_iota(jnp.int32, (span, 2 * span), 1)
+        query_ids = i * span + lax.broadcasted_iota(jnp.int32, (span, 2 * span), 0)
+        allowed = (key_ids >= first[i]) & (key_ids <= query_ids)
         for g in range(att.shape[1] // HEAD_DIM):
             cols = slice(g * HEAD_DIM, (g + 1) * HEAD_DIM)
             query = rotate(qacc[:, cols] * scale, i).astype(BF16)
             scores = lax.dot_general(
                 query, both[:, :HEAD_DIM], (((1,), (1,)), ((), ())), preferred_element_type=F32
             ) * (1.0 / math.sqrt(HEAD_DIM))
-            weights = jnp.where(mask[i] > 0.0, jnp.exp(scores), 0.0)
+            weights = jnp.where(allowed, jnp.exp(scores), 0.0)
             probs = (weights / jnp.sum(weights, axis=1, keepdims=True)).astype(BF16)
             att[:, cols] = dot(probs, both[:, HEAD_DIM:]).astype(BF16)
+
+        @pl.when(i == 0)
+        def _():
+            out_load.wait()
 
         def term(p, ci):
             cols = pl.ds(pl.multiple_of((p * chunks + ci) * block, block), block)
@@ -328,6 +364,10 @@
             def _():
                 spread(i + 1, ci - 1)
         loop(chunks + 1, finish)
+
+        @pl.when((layer == 0) & (i == 0))
+        def _():
+            loop(SUBS * chunks, send_rest)
 
         @pl.when(layer == last)
         def _():
@@ -445,17 +485,13 @@
     positions = (
         jnp.sum(jnp.where(req_onehot, (prior_offsets - req_starts)[None, :], 0), axis=1) + tok_ids
     )
-    spans = jnp.arange(SPLIT, dtype=jnp.int32)[:, None, None] * span
-    query_ids = spans + jnp.arange(span, dtype=jnp.int32)[None, :, None]
-    key_ids = spans + jnp.arange(-span, span, dtype=jnp.int32)[None, None, :]
-    first_ids = jnp.sum(jnp.where(req_onehot, req_starts[None, :], 0), axis=1).reshape(SPLIT, span, 1)
-    mask = ((key_ids >= first_ids) & (key_ids <= query_ids)).astype(F32)
+    first = jnp.sum(jnp.where(req_onehot, req_starts[None, :], 0), axis=1).reshape(SPLIT, span, 1)
     half = HEAD_DIM // 2
-    inv_freq = jnp.power(F32(ROPE_BASE), -(2.0 * jnp.arange(half, dtype=F32)) / HEAD_DIM)
-    angle = positions.astype(F32)[:, None] * inv_freq[None, :]
-    cos, sin = jnp.cos(angle), jnp.sin(angle)
-    cosf = jnp.concatenate([cos, cos], axis=1).reshape(SPLIT, span, HEAD_DIM)
-    sinf = jnp.concatenate([-sin, sin], axis=1).reshape(SPLIT, span, HEAD_DIM)
+    lanes = jnp.arange(HEAD_DIM, dtype=jnp.int32)
+    inv_freq = jnp.power(F32(ROPE_BASE), -(2.0 * (lanes % half).astype(F32)) / HEAD_DIM)
+    angle = positions.astype(F32).reshape(SPLIT, span, 1) * inv_freq
+    cosf = jnp.cos(angle)
+    sinf = jnp.sin(angle) * jnp.where(lanes < half, -1.0, 1.0)
 
     mine = jnp.arange(layers, dtype=jnp.int32) * SUBS + sub
     chosen = owners[None, :] == mine[:, None]
@@ -483,7 +519,7 @@
             jax.ShapeDtypeStruct((SUBS, chunks, tok_pad, block), BF16),
             jax.ShapeDtypeStruct((layers, cap_pad, 2 * HEAD_DIM), BF16),
         ),
-        in_specs=[pl.BlockSpec(memory_space=pltpu.VMEM)] * 10,
+        in_specs=[pl.BlockSpec(memory_space=pl.ANY)] * 5 + [pl.BlockSpec(memory_space=pltpu.VMEM)] * 5,
         out_specs=(pl.BlockSpec(memory_space=pltpu.VMEM),) * 2,
         scratch_shapes=[
             vm((SPLIT, pieces, chunks) + blk, BF16),
@@ -518,12 +554,18 @@
             dma((layers,)),
             dma((sections,)),
             dma((SUBS,)),
+            vm(hidden_t.shape, BF16),
+            vm(q_weight.shape[1:], BF16),
+            vm(k_weight.shape[1:], BF16),
+            vm(v_weight.shape[1:], BF16),
+            vm(o_weight.shape[1:], BF16),
+            dma((5,)),
         ],
         compiler_params=pltpu.CompilerParams(
             collective_id=0, has_side_effects=True, vmem_limit_bytes=56 * 1024 * 1024
         ),
         name="relay",
-    )(hidden_t, gain, q_weight[0], k_weight[0], v_weight[0], o_weight[0], cosf, sinf, mask, pick)
+    )(hidden_t, q_weight[0], k_weight[0], v_weight[0], o_weight[0], gain, cosf, sinf, first, pick)
     final_hidden = fin[:, :, :own_tokens].transpose(0, 1, 3, 2).reshape(rows_dev, own_tokens)
     return final_hidden, kv[None, :, :capacity]
 

time: 189 us -> 182 us (0.963)
  Pallas kernels: 178 us -> 171 us
    pallas_call x1, Pallas kernels: 178 us -> 171 us  [shards(): pl.pallas_call(functools.partial(relay_kernel, layers, tps, own_tokens),...]
where the time goes in v5:
time: 182 us
  Pallas kernels  171 us (94%)
  local copies, waits for them, and re-layouts  5.11 us (3%)
  other arithmetic  5.03 us (3%)
    pallas_call x1, Pallas kernels, shards(): pl.pallas_call(functools.partial(relay_kernel, layers, tps, own_tokens),...  171 us

profile of v5, /device:TPU:28, one launch (start us, length us, event | category | flops | bytes accessed | tf_op | source)
XLA Modules:
  0.0 181.9 jit_solution(13947584951743494088)
XLA Ops:
  0.6 0.0 copy-start
  0.7 0.7 copy.15
  1.5 0.1 reduce
  1.6 0.7 fusion.8
  2.3 0.9 fusion.2
  3.2 0.1 iota_compare_fusion.2
  3.2 0.1 convert_reduce_fusion
  3.3 0.1 select_reduce_fusion
  3.4 0.1 reduce_sum.49
  3.5 0.1 iota_add_fusion
  3.6 0.0 copy-done
  3.6 0.6 convert.1.gain
  4.3 0.8 and_convert_fusion.pick
  5.1 0.9 reshape.156.first
  6.0 1.5 fusion
  7.5 171.0 %relay.1 = (bf16[4,4,32,256]{3,2,1,0:T(8,128)(2,1)}, bf16[4,48,256]{2,1,0:T(8,128)(2,1)}) custom-call(bf16[4096,384]{1,0:T(8,128)(2,1)} %hin_hbm.1, bf16[8192,256]{1,0:T(8,128)(2,1)} %bitcast.12, bf16[2048,128]{1,0:T(8,128)(2,1)} %bitcast.14, bf16[2048,128]{1,0:T(8,128)(2,1)} %bitcast.15, bf16[256,8192]{1,0:T(8,128)(2,1)} %bitcast.13, ...), custom_call_target="tpu_custom_call" | custom-call | tf_op jit(solution)/shard_map/relay/pallas_call | solution.py:516
  178.5 0.9 slice_bitcast_fusion
  179.4 0.1 copy.17
  179.5 0.8 reshape.154
  180.3 1.5 copy.19
  (6 shorter events, 0.1 us)
Async XLA Ops:
  0.6 3.0 %copy-start = (bf16[4,8192]{1,0:T(4,128)(2,1)S(1)}, bf16[4,8192]{1,0:T(4,128)(2,1)}, u32[]{:S(2)}) copy-start(bf16[4,8192]{1,0:T(4,128)(2,1)} %param.10) | copy-start | bytes 196612

commit v6 on v5

--- a/solution.py
+++ b/solution.py
@@ -299,16 +299,6 @@
             return dot(att[...], wo[:, cols]).astype(BF16)
 
         def project(k):
-            @pl.when(k < chunks)
-            def _():
-                for e in range(1, tps):
-                    for r in (1, 2, 3, 0):
-                        s1out[i, r, k, e - 1] = term(sub_at(r) * tps + tp_at(e), k)
-                    for r in (1, 2, 3, 0):
-                        s1_copy(i, r, k, e).start()
-                for r in range(SUBS):
-                    s1own[i, r, k] = term(sub_at(r) * tps + t, k)
-
             @pl.when(k >= 1)
             def _():
                 ci = k - 1
@@ -320,6 +310,16 @@
                     s1own[i, r, ci] = total.astype(BF16)
                     if r > 0:
                         s2_copy(i, r, ci).start()
+
+            @pl.when(k < chunks)
+            def _():
+                for e in range(1, tps):
+                    for r in (1, 2, 3, 0):
+                        s1out[i, r, k, e - 1] = term(sub_at(r) * tps + tp_at(e), k)
+                    for r in (1, 2, 3, 0):
+                        s1_copy(i, r, k, e).start()
+                for r in range(SUBS):
+                    s1own[i, r, k] = term(sub_at(r) * tps + t, k)
         loop(chunks + 1, project)
 
         @pl.when(i == splits - 1)

time: 182 us -> 186 us (1.022)
  Pallas kernels: 171 us -> 175 us
    pallas_call x1, Pallas kernels: 171 us -> 175 us  [shards(): pl.pallas_call(functools.partial(relay_kernel, layers, tps, own_tokens),...]
where the time goes in v6:
time: 186 us
  Pallas kernels  175 us (94%)
  local copies, waits for them, and re-layouts  5.11 us (3%)
  other arithmetic  5.03 us (3%)
    pallas_call x1, Pallas kernels, shards(): pl.pallas_call(functools.partial(relay_kernel, layers, tps, own_tokens),...  175 us

profile of v6, /device:TPU:28, one launch (start us, length us, event | category | flops | bytes accessed | tf_op | source)
XLA Modules:
  0.0 185.7 jit_solution(11444513890476342161)
XLA Ops:
  0.6 0.0 copy-start
  0.7 0.7 copy.15
  1.5 0.1 reduce
  1.6 0.7 fusion.8
  2.3 0.9 fusion.2
  3.2 0.1 iota_compare_fusion.2
  3.2 0.1 convert_reduce_fusion
  3.3 0.1 select_reduce_fusion
  3.4 0.1 reduce_sum.49
  3.5 0.1 iota_add_fusion
  3.6 0.0 copy-done
  3.6 0.6 convert.1.gain
  4.3 0.8 and_convert_fusion.pick
  5.1 0.9 reshape.156.first
  6.0 1.5 fusion
  7.5 174.9 %relay.1 = (bf16[4,4,32,256]{3,2,1,0:T(8,128)(2,1)}, bf16[4,48,256]{2,1,0:T(8,128)(2,1)}) custom-call(bf16[4096,384]{1,0:T(8,128)(2,1)} %hin_hbm.1, bf16[8192,256]{1,0:T(8,128)(2,1)} %bitcast.12, bf16[2048,128]{1,0:T(8,128)(2,1)} %bitcast.14, bf16[2048,128]{1,0:T(8,128)(2,1)} %bitcast.15, bf16[256,8192]{1,0:T(8,128)(2,1)} %bitcast.13, ...), custom_call_target="tpu_custom_call" | custom-call | tf_op jit(solution)/shard_map/relay/pallas_call | solution.py:516
  182.4 0.9 slice_bitcast_fusion
  183.3 0.1 copy.17
  183.4 0.8 reshape.154
  184.2 1.5 copy.19
  (6 shorter events, 0.1 us)
Async XLA Ops:
  0.6 3.0 %copy-start = (bf16[4,8192]{1,0:T(4,128)(2,1)S(1)}, bf16[4,8192]{1,0:T(4,128)(2,1)}, u32[]{:S(2)}) copy-start(bf16[4,8192]{1,0:T(4,128)(2,1)} %param.10) | copy-start | bytes 196612
